TPU v7x, 32 devices: a whole 2x2x4 slice. The times are simulated.
32 devices in a mesh: section: 2 (over x), expert: 4 (over y, core), tensor: 4 (over z).
Axes of the slice: x: 2, y: 2, z: 4, core: 2. Of those that a mesh axis runs over, the one named last changes fastest.
Arguments:
- inputs: bfloat16 [2, 1024, 1024], P(None, 'expert'), may hold values from -6 to 6
- cotangent: bfloat16 [2, 1024, 1024], P(None, 'expert'), may hold values from -6 to 6
- seq_lengths: int32 [2, 16], P(None, 'expert'), may hold values from 0 to 256, as said below
- routes: int32 [2, 1024, 8], P(None, 'expert'), may hold values from 0 to 31, all different within a row; in each aligned block of 256 rows (0 to 255, 256 to 511, ..., all dimensions but the last counted through in order) at most 72 rows name the same one
- gain_attn: bfloat16 [2, 1024], P('section'), may hold values from 0.25 to 1.75
- w_query: bfloat16 [2, 1024, 1024], P('section', None, 'tensor'), may hold values from -0.1875 to 0.1875
- key_projection: bfloat16 [2, 1024, 512], P('section', None, 'tensor'), may hold values from -0.1875 to 0.1875
- value_projection: bfloat16 [2, 1024, 512], P('section', None, 'tensor'), may hold values from -0.1875 to 0.1875
- w_out: bfloat16 [2, 1024, 1024], P('section', 'tensor'), may hold values from -0.75 to 0.75
- gain_moe: bfloat16 [2, 1024], P('section'), may hold values from 0.25 to 1.75
- w_router: bfloat16 [2, 1024, 32], P('section'), may hold values from -0.09375 to 0.09375
- w_gate: bfloat16 [2, 32, 1024, 512], P('section', 'expert', None, 'tensor'), may hold values from -0.1875 to 0.1875
- w_up: bfloat16 [2, 32, 1024, 512], P('section', 'expert', None, 'tensor'), may hold values from -0.1875 to 0.1875
- w_down: bfloat16 [2, 32, 512, 1024], P('section', 'expert', 'tensor'), may hold values from -1 to 1
Outputs:
- activations: bfloat16 [2, 2, 1024, 1024], P('section', None, 'expert')
- input_grads: bfloat16 [2, 2, 1024, 1024], P('section', None, 'expert')
- grad_gain_attn: float32 [2, 1024], P('section')
- grad_query: float32 [2, 1024, 1024], P('section', None, 'tensor')
- grad_key: float32 [2, 1024, 512], P('section', None, 'tensor')
- grad_value: float32 [2, 1024, 512], P('section', None, 'tensor')
- grad_out: float32 [2, 1024, 1024], P('section', 'tensor')
- grad_gain_moe: float32 [2, 1024], P('section')
- grad_router: float32 [2, 1024, 32], P('section')
- grad_gate: float32 [2, 32, 1024, 512], P('section', 'expert', None, 'tensor')
- grad_up: float32 [2, 32, 1024, 512], P('section', 'expert', None, 'tensor')
- grad_down: float32 [2, 32, 512, 1024], P('section', 'expert', 'tensor')
Inputs may be any that keep to these rules, and one draw needn't show every extreme that they name: `seq_lengths`: for each micro-batch and each index of the expert axis the 4 lengths sum to between 128 and 256; in every micro-batch one index holds a single sequence of all 256 rows and zeros in its other entries. `routes`: each row names 8 different experts. Within the rows of one index of the expert axis in one micro-batch no expert is named by more than 72 rows, and in some of these blocks one expert is named by exactly 72.
All inputs are finite; a program needn't handle non-finite values.
Results may differ from a plain program's by a relative error of at most 0.025.
Values may be sent and summed in bfloat16 or wider, within the bound.
No kernel may reach another device: no remote copies, remote signals or barrier semaphores. Data moves between devices by JAX's collectives and lax.ppermute only.
A program may use at most 256 MiB of HBM per device.

v0:
```python
import jax
import jax.numpy as jnp
from jax import lax
from jax.sharding import PartitionSpec as P

QUERY_HEADS = 16
KEY_VALUE_HEADS = 8
HEAD_SIZE = 64
NE = 32
TOPK = 8
TOKEN_ROWS = 256
SLOTS = 4
CAP = 72


EPSILON = 1e-06
THETA_BASE = 10000.0
MASKED = -1e30


def shifted(array, axis, by):
    length = lax.axis_size(axis)
    pairs = [(i, i + by) for i in range(length) if 0 <= i + by < length]
    return lax.ppermute(array, axis, pairs)


def rms_scale(values):
    return lax.rsqrt(jnp.mean(values * values, axis=-1, keepdims=True) + EPSILON)


def norm_backward(grad_normed, values, scale_rows, gain):
    grad_gain = jnp.sum(grad_normed * values * scale_rows, axis=0)
    weighted = grad_normed * gain
    grad_values = scale_rows * weighted - values * scale_rows**3 * jnp.mean(
        values * weighted, axis=-1, keepdims=True
    )
    return (grad_gain, grad_values)


def layout(lengths, row_count, slot_count):
    row_ids = jnp.arange(row_count, dtype=jnp.int32)
    seq_ends = jnp.cumsum(lengths)
    starts = jnp.concatenate([seq_ends - lengths, seq_ends[-1:]])
    segment = jnp.sum((row_ids[:, None] >= seq_ends[None, :]).astype(jnp.int32), axis=1)
    picked = segment[:, None] == jnp.arange(slot_count + 1, dtype=jnp.int32)[None, :]
    begins = jnp.sum(jnp.where(picked, starts[None, :], 0), axis=1)
    return (segment, (row_ids - begins).astype(jnp.float32))


def tables(position, head_dim):
    frequency = THETA_BASE ** (-jnp.arange(0, head_dim, 2, dtype=jnp.float32) / head_dim)
    angles = position[:, None] * frequency[None, :]
    cosine_lookup = jnp.concatenate([jnp.cos(angles), jnp.cos(angles)], axis=-1)[:, None, :]
    sine_lookup = jnp.concatenate([jnp.sin(angles), jnp.sin(angles)], axis=-1)[:, None, :]
    return (cosine_lookup, sine_lookup)


def rotary_apply(values, cosine_lookup, sine_lookup):
    half_dim = values.shape[-1] // 2
    turned = jnp.concatenate([-values[..., half_dim:], values[..., :half_dim]], axis=-1)
    return values * cosine_lookup + turned * sine_lookup


def unrotate(grads, cosine_lookup, sine_lookup):
    scaled = grads * sine_lookup
    half_dim = grads.shape[-1] // 2
    turned = jnp.concatenate([-scaled[..., half_dim:], scaled[..., :half_dim]], axis=-1)
    return grads * cosine_lookup - turned


def slot_tables(route_ids, live_rows, expert_count, capacity):
    row_count, top_count = route_ids.shape
    flat_ids = route_ids.reshape(-1)
    keeping = jnp.repeat(live_rows, top_count)
    hits = (
        (flat_ids[:, None] == jnp.arange(expert_count, dtype=jnp.int32)[None, :]) & keeping[:, None]
    ).astype(jnp.int32)
    before = jnp.cumsum(hits, axis=0) - hits
    place = jnp.sum(before * hits, axis=1)
    owner = jnp.where(keeping, flat_ids, expert_count)
    pair_count = row_count * top_count
    table = jnp.full((expert_count, capacity), pair_count, jnp.int32)
    table = table.at[owner, place].set(jnp.arange(pair_count, dtype=jnp.int32), mode="drop")
    return (owner, place, table)


def attend_forward(query_matrix, key_rows, value_rows, segment, score_scale, block_rows):
    row_count = query_matrix.shape[0]
    row_ids = jnp.arange(row_count, dtype=jnp.int32)

    def one_block(block_no):
        allowed = (segment[:, None] == segment[None, :]) & (row_ids[None, :] <= row_ids[:, None])
        scores = (
            jnp.einsum("qhgd,khd->hgqk", query_matrix, key_rows, preferred_element_type=jnp.float32)
            * score_scale
        )
        scores = jnp.where(allowed, scores, MASKED)
        row_peak = jnp.max(scores, axis=-1, keepdims=True)
        exp_scores = jnp.exp(scores - row_peak)
        row_total = jnp.sum(exp_scores, axis=-1, keepdims=True)
        probs = exp_scores / row_total
        mixed = jnp.einsum(
            "hgqk,khd->qhgd",
            probs.astype(jnp.bfloat16),
            value_rows,
            preferred_element_type=jnp.float32,
        )
        return (mixed, (row_peak + jnp.log(row_total))[..., 0])

    mixed, log_sums = lax.map(one_block, jnp.arange(row_count // block_rows, dtype=jnp.int32))
    return (mixed.reshape(query_matrix.shape), log_sums)


def attend_backward(
    grad_mixed, query_matrix, key_rows, value_rows, segment, log_sums, score_scale, block_rows
):
    row_count = query_matrix.shape[0]
    row_ids = jnp.arange(row_count, dtype=jnp.int32)

    def one_block(carry, block_no):
        grad_keys, grad_values = carry
        log_blk = lax.dynamic_index_in_dim(log_sums, block_no, 0, keepdims=False)
        allowed = (segment[:, None] == segment[None, :]) & (row_ids[None, :] <= row_ids[:, None])
        scores = (
            jnp.einsum("qhgd,khd->hgqk", query_matrix, key_rows, preferred_element_type=jnp.float32)
            * score_scale
        )
        scores = jnp.where(allowed, scores, MASKED)
        probs = jnp.exp(scores - log_blk[..., None])
        grad_probs = jnp.einsum(
            "qhgd,khd->hgqk", grad_mixed, value_rows, preferred_element_type=jnp.float32
        )
        inner = jnp.sum(probs * grad_probs, axis=-1, keepdims=True)
        grad_scores = (probs * (grad_probs - inner)).astype(jnp.bfloat16)
        grad_query = (
            jnp.einsum("hgqk,khd->qhgd", grad_scores, key_rows, preferred_element_type=jnp.float32)
            * score_scale
        )
        grad_keys = (
            grad_keys
            + jnp.einsum(
                "hgqk,qhgd->khd", grad_scores, query_matrix, preferred_element_type=jnp.float32
            )
            * score_scale
        )
        grad_values = grad_values + jnp.einsum(
            "hgqk,qhgd->khd",
            probs.astype(jnp.bfloat16),
            grad_mixed,
            preferred_element_type=jnp.float32,
        )
        return ((grad_keys, grad_values), grad_query)

    zeros_kv = jnp.zeros(key_rows.shape, jnp.float32)
    (grad_keys, grad_values), grad_query = lax.scan(
        one_block, (zeros_kv, zeros_kv), jnp.arange(row_count // block_rows, dtype=jnp.int32)
    )
    return (grad_query.reshape(query_matrix.shape), grad_keys, grad_values)


def expert_forward(expert_rows, w_g, w_u, w_d):
    gate_h = jnp.einsum("erd,edf->erf", expert_rows, w_g, preferred_element_type=jnp.float32)
    up_h = jnp.einsum("erd,edf->erf", expert_rows, w_u, preferred_element_type=jnp.float32)
    hidden = (jax.nn.silu(gate_h) * up_h).astype(jnp.bfloat16)
    part = jnp.einsum("erf,efd->erd", hidden, w_d, preferred_element_type=jnp.float32).astype(
        jnp.bfloat16
    )
    return (gate_h, up_h, hidden, part)


def expert_backward(grad_part, expert_rows, gate_h, up_h, hidden, w_g, w_u, w_d):
    grad_wd = jnp.einsum("erf,erd->efd", hidden, grad_part, preferred_element_type=jnp.float32)
    grad_hidden = jnp.einsum("erd,efd->erf", grad_part, w_d, preferred_element_type=jnp.float32)
    sig_gate = jax.nn.sigmoid(gate_h)
    grad_gate = (grad_hidden * up_h * sig_gate * (1.0 + gate_h * (1.0 - sig_gate))).astype(
        jnp.bfloat16
    )
    grad_up = (grad_hidden * gate_h * sig_gate).astype(jnp.bfloat16)
    grad_wg = jnp.einsum("erd,erf->edf", expert_rows, grad_gate, preferred_element_type=jnp.float32)
    grad_wu = jnp.einsum("erd,erf->edf", expert_rows, grad_up, preferred_element_type=jnp.float32)
    grad_rows = jnp.einsum("erf,edf->erd", grad_gate, w_g, preferred_element_type=jnp.float32)
    grad_rows = grad_rows + jnp.einsum(
        "erf,edf->erd", grad_up, w_u, preferred_element_type=jnp.float32
    )
    return (grad_rows.astype(jnp.bfloat16), grad_wg, grad_wu, grad_wd)


def to_experts(slot_rows):
    rank_count = lax.axis_size("expert")
    local_count = slot_rows.shape[0] // rank_count
    feature_count = slot_rows.shape[2]
    arrived = lax.all_to_all(
        slot_rows.reshape(rank_count, local_count, slot_rows.shape[1], feature_count),
        "expert",
        split_axis=0,
        concat_axis=2,
        tiled=True,
    )
    return arrived.reshape(local_count, rank_count * slot_rows.shape[1], feature_count)


def from_experts(expert_out):
    rank_count = lax.axis_size("expert")
    local_count = expert_out.shape[0]
    slot_count = expert_out.shape[1] // rank_count
    arrived = lax.all_to_all(
        expert_out.reshape(local_count, rank_count, slot_count, expert_out.shape[2]),
        "expert",
        split_axis=1,
        concat_axis=0,
        tiled=True,
    )
    return arrived.reshape(local_count * rank_count, slot_count, expert_out.shape[2])


def layer_forward(layer_in, weights, lengths, route_ids):
    gain_a, w_q, key_weight, value_weight, w_o, gain_m, w_r, w_g, w_u, w_d = weights
    kv_heads = key_weight.shape[-1] // HEAD_SIZE
    query_groups = QUERY_HEADS // KEY_VALUE_HEADS
    segment, position = layout(lengths, TOKEN_ROWS, SLOTS)
    live_rows = segment < SLOTS
    cosine_lookup, sine_lookup = tables(position, HEAD_SIZE)
    resid = layer_in.astype(jnp.float32)
    scale_in = rms_scale(resid)
    normalized_input = (resid * scale_in * gain_a).astype(jnp.bfloat16)
    query_matrix = rotary_apply(
        jnp.dot(normalized_input, w_q, preferred_element_type=jnp.float32).reshape(
            TOKEN_ROWS, kv_heads * query_groups, HEAD_SIZE
        ),
        cosine_lookup,
        sine_lookup,
    )
    query_matrix = query_matrix.astype(jnp.bfloat16).reshape(
        TOKEN_ROWS, kv_heads, query_groups, HEAD_SIZE
    )
    key_rows = rotary_apply(
        jnp.dot(normalized_input, key_weight, preferred_element_type=jnp.float32).reshape(
            TOKEN_ROWS, kv_heads, HEAD_SIZE
        ),
        cosine_lookup,
        sine_lookup,
    ).astype(jnp.bfloat16)
    value_rows = (
        jnp.dot(normalized_input, value_weight, preferred_element_type=jnp.float32)
        .astype(jnp.bfloat16)
        .reshape(TOKEN_ROWS, kv_heads, HEAD_SIZE)
    )
    mixed, log_sums = attend_forward(
        query_matrix, key_rows, value_rows, segment, HEAD_SIZE ** (-0.5), min(512, TOKEN_ROWS)
    )
    attended = mixed.reshape(TOKEN_ROWS, kv_heads * query_groups * HEAD_SIZE).astype(jnp.bfloat16)
    attn_term = lax.psum(jnp.dot(attended, w_o, preferred_element_type=jnp.float32), "tensor")
    middle = resid + attn_term
    scale_mid = rms_scale(middle)
    normed_mid = (middle * scale_mid * gain_m).astype(jnp.bfloat16)
    logits = jnp.dot(normed_mid, w_r, preferred_element_type=jnp.float32)
    chooser = route_ids[:, :, None] == jnp.arange(NE, dtype=jnp.int32)[None, None, :]
    softmaxed = jax.nn.softmax(
        jnp.sum(jnp.where(chooser, logits[:, None, :], 0.0), axis=-1), axis=-1
    )
    gates = softmaxed * live_rows.astype(jnp.float32)[:, None]
    owner, place, table = slot_tables(route_ids, live_rows, NE, CAP)
    valid = table < TOKEN_ROWS * TOPK
    source = jnp.minimum(table // TOPK, TOKEN_ROWS - 1)
    dispatched = jnp.where(valid[:, :, None], normed_mid[source], jnp.zeros((), jnp.bfloat16))
    expert_rows = to_experts(dispatched)
    gate_h, up_h, hidden, part = expert_forward(expert_rows, w_g, w_u, w_d)
    returned = from_experts(part)
    slot_index = jnp.minimum(owner, NE - 1) * CAP + place
    picked = returned.reshape(NE * CAP, -1)[slot_index].reshape(TOKEN_ROWS, TOPK, -1)
    moe_term = lax.psum(
        jnp.einsum("rk,rkd->rd", gates, picked, preferred_element_type=jnp.float32), "tensor"
    )
    layer_out = (middle + moe_term).astype(jnp.bfloat16)
    saved = (
        resid,
        scale_in,
        normalized_input,
        query_matrix,
        key_rows,
        value_rows,
        log_sums,
        attended,
        middle,
        scale_mid,
        normed_mid,
        softmaxed,
        live_rows,
        chooser,
        owner,
        place,
        table,
        expert_rows,
        gate_h,
        up_h,
        hidden,
        returned,
        cosine_lookup,
        sine_lookup,
        segment,
    )
    return (layer_out, saved)


def layer_backward(grad_out, saved, weights):
    (
        resid,
        scale_in,
        normalized_input,
        query_matrix,
        key_rows,
        value_rows,
        log_sums,
        attended,
        middle,
        scale_mid,
        normed_mid,
        softmaxed,
        live_rows,
        chooser,
        owner,
        place,
        table,
        expert_rows,
        gate_h,
        up_h,
        hidden,
        returned,
        cosine_lookup,
        sine_lookup,
        segment,
    ) = saved
    gain_a, w_q, key_weight, value_weight, w_o, gain_m, w_r, w_g, w_u, w_d = weights
    kv_heads = key_weight.shape[-1] // HEAD_SIZE
    query_groups = QUERY_HEADS // KEY_VALUE_HEADS
    grad_y = grad_out.astype(jnp.float32)
    live_float = live_rows.astype(jnp.float32)[:, None]
    gates = softmaxed * live_float
    valid = table < TOKEN_ROWS * TOPK
    source = jnp.minimum(table // TOPK, TOKEN_ROWS - 1)
    pair_gate = jnp.where(valid, gates.reshape(-1)[jnp.minimum(table, TOKEN_ROWS * TOPK - 1)], 0.0)
    grad_dispatch = (grad_y[source] * pair_gate[:, :, None]).astype(jnp.bfloat16)
    grad_part = to_experts(grad_dispatch)
    grad_rows_e, grad_wg, grad_wu, grad_wd = expert_backward(
        grad_part, expert_rows, gate_h, up_h, hidden, w_g, w_u, w_d
    )
    grad_back = from_experts(grad_rows_e)
    slot_index = jnp.minimum(owner, NE - 1) * CAP + place
    grad_picked = grad_back.reshape(NE * CAP, -1)[slot_index].reshape(TOKEN_ROWS, TOPK, -1)
    picked = returned.reshape(NE * CAP, -1)[slot_index].reshape(TOKEN_ROWS, TOPK, -1)
    grad_mid_part = jnp.sum(grad_picked.astype(jnp.float32), axis=1) * live_float
    grad_gate_part = jnp.einsum("rd,rkd->rk", grad_y, picked, preferred_element_type=jnp.float32)
    grad_mid_moe, grad_gates = lax.psum((grad_mid_part, grad_gate_part), "tensor")
    grad_soft = grad_gates * live_float
    grad_chosen = softmaxed * (grad_soft - jnp.sum(softmaxed * grad_soft, axis=-1, keepdims=True))
    grad_logits = jnp.sum(jnp.where(chooser, grad_chosen[:, :, None], 0.0), axis=1).astype(
        jnp.bfloat16
    )
    grad_wr = jnp.einsum("rd,re->de", normed_mid, grad_logits, preferred_element_type=jnp.float32)
    grad_normed_mid = grad_mid_moe + jnp.einsum(
        "re,de->rd", grad_logits, w_r, preferred_element_type=jnp.float32
    )
    grad_gain_m, grad_middle = norm_backward(grad_normed_mid, middle, scale_mid, gain_m)
    grad_middle = grad_middle + grad_y
    grad_mid_b = grad_middle.astype(jnp.bfloat16)
    grad_wo = jnp.einsum("rc,rd->cd", attended, grad_mid_b, preferred_element_type=jnp.float32)
    grad_mixed = (
        jnp.einsum("rd,cd->rc", grad_mid_b, w_o, preferred_element_type=jnp.float32)
        .astype(jnp.bfloat16)
        .reshape(TOKEN_ROWS, kv_heads, query_groups, HEAD_SIZE)
    )
    grad_query, grad_keys, grad_values = attend_backward(
        grad_mixed,
        query_matrix,
        key_rows,
        value_rows,
        segment,
        log_sums,
        HEAD_SIZE ** (-0.5),
        min(512, TOKEN_ROWS),
    )
    grad_query = (
        unrotate(
            grad_query.reshape(TOKEN_ROWS, kv_heads * query_groups, HEAD_SIZE),
            cosine_lookup,
            sine_lookup,
        )
        .reshape(TOKEN_ROWS, -1)
        .astype(jnp.bfloat16)
    )
    grad_keys = (
        unrotate(grad_keys, cosine_lookup, sine_lookup).reshape(TOKEN_ROWS, -1).astype(jnp.bfloat16)
    )
    grad_values = grad_values.reshape(TOKEN_ROWS, -1).astype(jnp.bfloat16)
    grad_wq = jnp.einsum(
        "rd,rc->dc", normalized_input, grad_query, preferred_element_type=jnp.float32
    )
    grad_wk = jnp.einsum(
        "rd,rc->dc", normalized_input, grad_keys, preferred_element_type=jnp.float32
    )
    grad_wv = jnp.einsum(
        "rd,rc->dc", normalized_input, grad_values, preferred_element_type=jnp.float32
    )
    grad_normed_part = jnp.einsum("rc,dc->rd", grad_query, w_q, preferred_element_type=jnp.float32)
    grad_normed_part = grad_normed_part + jnp.einsum(
        "rc,dc->rd", grad_keys, key_weight, preferred_element_type=jnp.float32
    )
    grad_normed_part = grad_normed_part + jnp.einsum(
        "rc,dc->rd", grad_values, value_weight, preferred_element_type=jnp.float32
    )
    grad_normed_in = lax.psum(grad_normed_part, "tensor")
    grad_gain_a, grad_in = norm_backward(grad_normed_in, resid, scale_in, gain_a)
    return (
        grad_in + grad_middle,
        (
            grad_gain_a,
            grad_wq,
            grad_wk,
            grad_wv,
            grad_wo,
            grad_gain_m,
            grad_wr,
            grad_wg,
            grad_wu,
            grad_wd,
        ),
    )


def local(
    inputs,
    cotangent,
    seq_lengths,
    routes,
    gain_attn,
    w_query,
    key_projection,
    value_projection,
    w_out,
    gain_moe,
    w_router,
    w_gate,
    w_up,
    w_down,
):
    section_no = lax.axis_index("section")
    first_section = section_no == 0
    micro_count = inputs.shape[0]
    expert_gate, expert_up, expert_down = (w_gate[0], w_up[0], w_down[0])
    weights = (
        gain_attn[0],
        w_query[0],
        key_projection[0],
        value_projection[0],
        w_out[0],
        gain_moe[0],
        w_router[0],
        expert_gate,
        expert_up,
        expert_down,
    )
    incoming = jnp.zeros_like(inputs[0])
    kept = []
    produced = []
    for tick_no in range(micro_count + 1):
        batch_no = jnp.clip(tick_no - section_no, 0, micro_count - 1)
        layer_in = jnp.where(first_section, inputs[min(tick_no, micro_count - 1)], incoming)
        layer_out, saved = layer_forward(layer_in, weights, seq_lengths[batch_no], routes[batch_no])
        kept.append(layer_in)
        produced.append(layer_out)
        if tick_no < micro_count:
            incoming = shifted(layer_out, "section", 1)
    returning = jnp.zeros_like(inputs[0])
    totals = None
    returned_grads = []
    for tick_no in range(micro_count + 1):
        offset = tick_no - 1 + section_no
        batch_no = jnp.clip(offset, 0, micro_count - 1)
        in_use = (offset >= 0) & (offset < micro_count)
        grad_out = jnp.where(first_section, returning, cotangent[min(tick_no, micro_count - 1)])
        stored = jnp.where(
            first_section, kept[max(tick_no - 1, 0)], kept[min(tick_no + 1, micro_count)]
        )
        saved = layer_forward(stored, weights, seq_lengths[batch_no], routes[batch_no])[1]
        grad_in, grads = layer_backward(grad_out, saved, weights)
        grads = tuple((jnp.where(in_use, member, 0.0) for member in grads))
        if totals is None:
            totals = grads
        else:
            totals = tuple((left_val + right_val for left_val, right_val in zip(totals, grads)))
        returned_grads.append(grad_in)
        if tick_no < micro_count:
            returning = shifted(grad_in.astype(jnp.bfloat16), "section", -1)
    shared = (
        lax.psum(totals[0].astype(jnp.bfloat16), "expert").astype(jnp.float32),
        lax.psum(totals[1].astype(jnp.bfloat16), "expert").astype(jnp.float32),
        lax.psum(totals[2].astype(jnp.bfloat16), "expert").astype(jnp.float32),
        lax.psum(totals[3].astype(jnp.bfloat16), "expert").astype(jnp.float32),
        lax.psum(totals[4].astype(jnp.bfloat16), "expert").astype(jnp.float32),
        lax.psum(totals[5].astype(jnp.bfloat16), "expert").astype(jnp.float32),
        lax.psum(totals[6].astype(jnp.bfloat16), "expert").astype(jnp.float32),
    )
    grad_gate_out, grad_up_out, grad_down_out = (totals[7], totals[8], totals[9])
    activations = jnp.stack(
        [
            jnp.where(first_section, produced[batch_idx], produced[batch_idx + 1])
            for batch_idx in range(micro_count)
        ]
    )
    input_grads = jnp.stack(
        [
            jnp.where(first_section, returned_grads[batch_idx + 1], returned_grads[batch_idx])
            for batch_idx in range(micro_count)
        ]
    ).astype(jnp.bfloat16)
    return (
        activations[None],
        input_grads[None],
        shared[0][None],
        shared[1][None],
        shared[2][None],
        shared[3][None],
        shared[4][None],
        shared[5][None],
        shared[6][None],
        grad_gate_out[None],
        grad_up_out[None],
        grad_down_out[None],
    )


def solution(mesh):
    in_specs = (
        P(None, "expert", None),
        P(None, "expert", None),
        P(None, "expert"),
        P(None, "expert", None),
        P("section", None),
        P("section", None, "tensor"),
        P("section", None, "tensor"),
        P("section", None, "tensor"),
        P("section", "tensor", None),
        P("section", None),
        P("section", None, None),
        P("section", "expert", None, "tensor"),
        P("section", "expert", None, "tensor"),
        P("section", "expert", "tensor", None),
    )
    out_specs = (
        P("section", None, "expert", None),
        P("section", None, "expert", None),
        P("section", None),
        P("section", None, "tensor"),
        P("section", None, "tensor"),
        P("section", None, "tensor"),
        P("section", "tensor", None),
        P("section", None),
        P("section", None, None),
        P("section", "expert", None, "tensor"),
        P("section", "expert", None, "tensor"),
        P("section", "expert", "tensor", None),
    )
    return jax.shard_map(local, mesh=mesh, in_specs=in_specs, out_specs=out_specs, check_vma=False)
```

profile of v0, /device:TPU:0, one launch (start us, length us, event | category | flops | bytes accessed | tf_op | source)
XLA Modules:
  0.0 2142.1 jit_solution(8537643150829080306)
XLA Ops:
  174.7 57.8 %all_to_all.270 = bf16[4,8,72,1024]{3,2,1,0:T(8,128)(2,1)S(1)} all-to-all(bf16[4,8,72,1024]{3,2,1,0:T(8,128)(2,1)S(1)} %broadcast_select_fusion.5), channel_id=1, replica_groups=mesh['section'=2,'expert'=4,'tensor'=4] {'expert'}, dimensions={0} | all-to-all | bytes 9437184 | tf_op jit(solution)/shard_map/all_to_all | solution.py:192
  257.8 52.5 %all-to-all-done.1 = bf16[8,4,72,1024]{3,2,0,1:T(8,128)(2,1)} async-done(((bf16[8,4,72,1024]{3,2,0,1:T(8,128)(2,1)}), bf16[8,4,72,1024]{3,2,0,1:T(8,128)(2,1)}, u32[]{:S(2)}, u32[]{:S(2)}) %all-to-all-start.1) | async-done | bytes 4718624 | tf_op jit(solution)/shard_map/all_to_all | solution.py:206
  330.9 50.3 %all-reduce.21.cloned.1.call-done = f32[256,1024]{1,0:T(8,128)} async-done(((f32[256,1024]{1,0:T(8,128)}), f32[256,1024]{1,0:T(8,128)}) %all-reduce.21.cloned.1.call-update) | async-done | bytes 1048592 | tf_op jit(solution)/shard_map/psum | solution.py:271
  443.2 67.8 %all-reduce.35.cloned.1.call-done = (f32[256,1024]{1,0:T(8,128)}, f32[256,1024]{1,0:T(8,128)}) async-done(((f32[256,1024]{1,0:T(8,128)}, f32[256,1024]{1,0:T(8,128)}), (f32[256,1024]{1,0:T(8,128)}, f32[256,1024]{1,0:T(8,128)})) %all-reduce.35.cloned.1.call-update) | async-done | bytes 2097168 | tf_op jit(solution)/shard_map/psum | solution.py:252
  553.1 41.5 %all-to-all-done.6 = bf16[4,8,72,1024]{3,2,1,0:T(8,128)(2,1)} async-done(((bf16[4,8,72,1024]{3,2,1,0:T(8,128)(2,1)}), bf16[4,8,72,1024]{3,2,1,0:T(8,128)(2,1)}, u32[]{:S(2)}, u32[]{:S(2)}) %all-to-all-start.6) | async-done | bytes 4718624 | tf_op jit(solution)/shard_map/all_to_all | solution.py:192
  620.3 33.2 %all-to-all-done.7 = bf16[4,8,72,1024]{3,2,1,0:T(8,128)(2,1)} async-done(((bf16[4,8,72,1024]{3,2,1,0:T(8,128)(2,1)}), bf16[4,8,72,1024]{3,2,1,0:T(8,128)(2,1)}, u32[]{:S(2)}, u32[]{:S(2)}) %all-to-all-start.7) | async-done | bytes 4718624 | tf_op jit(solution)/shard_map/all_to_all | solution.py:192
  679.1 33.4 %all-to-all-done.2 = bf16[4,8,72,1024]{3,2,1,0:T(8,128)(2,1)} async-done(((bf16[4,8,72,1024]{3,2,1,0:T(8,128)(2,1)}), bf16[4,8,72,1024]{3,2,1,0:T(8,128)(2,1)}, u32[]{:S(2)}, u32[]{:S(2)}) %all-to-all-start.2) | async-done | bytes 4718624 | tf_op jit(solution)/shard_map/all_to_all | solution.py:192
  738.7 32.8 %all-to-all-done.8 = bf16[8,4,72,1024]{3,2,0,1:T(8,128)(2,1)} async-done(((bf16[8,4,72,1024]{3,2,0,1:T(8,128)(2,1)}), bf16[8,4,72,1024]{3,2,0,1:T(8,128)(2,1)}, u32[]{:S(2)}, u32[]{:S(2)}) %all-to-all-start.8) | async-done | bytes 4718624 | tf_op jit(solution)/shard_map/all_to_all | solution.py:206
  782.4 48.0 %all-to-all-done.3 = bf16[8,4,72,1024]{3,2,0,1:T(8,128)(2,1)} async-done(((bf16[8,4,72,1024]{3,2,0,1:T(8,128)(2,1)}), bf16[8,4,72,1024]{3,2,0,1:T(8,128)(2,1)}, u32[]{:S(2)}, u32[]{:S(2)}) %all-to-all-start.3) | async-done | bytes 4718624 | tf_op jit(solution)/shard_map/all_to_all | solution.py:206
  918.9 43.7 %all-reduce.33.cloned.1.call-done = (f32[256,1024]{1,0:T(8,128)}, f32[256,1024]{1,0:T(8,128)}) async-done(((f32[256,1024]{1,0:T(8,128)}, f32[256,1024]{1,0:T(8,128)}), (f32[256,1024]{1,0:T(8,128)}, f32[256,1024]{1,0:T(8,128)})) %all-reduce.33.cloned.1.call-update) | async-done | bytes 2097168 | tf_op jit(solution)/shard_map/psum | solution.py:271
  1005.0 76.5 %all-reduce.31.cloned.1.call-done = (f32[256,1024]{1,0:T(8,128)}, f32[256,1024]{1,0:T(8,128)}) async-done(((f32[256,1024]{1,0:T(8,128)}, f32[256,1024]{1,0:T(8,128)}), (f32[256,1024]{1,0:T(8,128)}, f32[256,1024]{1,0:T(8,128)})) %all-reduce.31.cloned.1.call-update) | async-done | bytes 2097168 | tf_op jit(solution)/shard_map/psum | solution.py:252
  1154.1 17.8 all-to-all-done.11
  1184.8 46.3 %all-to-all-done.10 = bf16[4,8,72,1024]{3,2,1,0:T(8,128)(2,1)} async-done(((bf16[4,8,72,1024]{3,2,1,0:T(8,128)(2,1)}), bf16[4,8,72,1024]{3,2,1,0:T(8,128)(2,1)}, u32[]{:S(2)}, u32[]{:S(2)}) %all-to-all-start.10) | async-done | bytes 4718624 | tf_op jit(solution)/shard_map/all_to_all | solution.py:192
  1259.4 45.6 %all-to-all-done.12 = bf16[8,4,72,1024]{3,2,0,1:T(8,128)(2,1)} async-done(((bf16[8,4,72,1024]{3,2,0,1:T(8,128)(2,1)}), bf16[8,4,72,1024]{3,2,0,1:T(8,128)(2,1)}, u32[]{:S(2)}, u32[]{:S(2)}) %all-to-all-start.12) | async-done | bytes 4718624 | tf_op jit(solution)/shard_map/all_to_all | solution.py:206
  1340.7 23.0 %all-to-all-done.13 = bf16[8,4,72,1024]{3,2,0,1:T(8,128)(2,1)} async-done(((bf16[8,4,72,1024]{3,2,0,1:T(8,128)(2,1)}), bf16[8,4,72,1024]{3,2,0,1:T(8,128)(2,1)}, u32[]{:S(2)}, u32[]{:S(2)}) %all-to-all-start.13) | async-done | bytes 4718624 | tf_op jit(solution)/shard_map/all_to_all | solution.py:206
  1416.1 76.4 %all-reduce.29.cloned.1.call-done = (f32[256,1024]{1,0:T(8,128)}, f32[256,1024]{1,0:T(8,128)}) async-done(((f32[256,1024]{1,0:T(8,128)}, f32[256,1024]{1,0:T(8,128)}), (f32[256,1024]{1,0:T(8,128)}, f32[256,1024]{1,0:T(8,128)})) %all-reduce.29.cloned.1.call-update) | async-done | bytes 2097168 | tf_op jit(solution)/shard_map/psum | solution.py:411
  1533.4 14.9 collective-permute-done.3
  1564.1 16.9 all-to-all-done.15
  1605.4 34.4 %all-to-all-done.14 = bf16[4,8,72,1024]{3,2,1,0:T(8,128)(2,1)} async-done(((bf16[4,8,72,1024]{3,2,1,0:T(8,128)(2,1)}), bf16[4,8,72,1024]{3,2,1,0:T(8,128)(2,1)}, u32[]{:S(2)}, u32[]{:S(2)}) %all-to-all-start.14) | async-done | bytes 4718624 | tf_op jit(solution)/shard_map/all_to_all | solution.py:192
  1686.2 28.6 %all-to-all-done.16 = bf16[8,4,72,1024]{3,2,0,1:T(8,128)(2,1)} async-done(((bf16[8,4,72,1024]{3,2,0,1:T(8,128)(2,1)}), bf16[8,4,72,1024]{3,2,0,1:T(8,128)(2,1)}, u32[]{:S(2)}, u32[]{:S(2)}) %all-to-all-start.16) | async-done | bytes 4718624 | tf_op jit(solution)/shard_map/all_to_all | solution.py:206
  1802.3 35.7 %all-reduce.27.cloned.1.call-done = (f32[256,1024]{1,0:T(8,128)}, f32[256,1024]{1,0:T(8,128)}) async-done(((f32[256,1024]{1,0:T(8,128)}, f32[256,1024]{1,0:T(8,128)}), (f32[256,1024]{1,0:T(8,128)}, f32[256,1024]{1,0:T(8,128)})) %all-reduce.27.cloned.1.call-update) | async-done | bytes 2097168 | tf_op jit(solution)/shard_map/psum | solution.py:252
  1876.7 38.7 %all-to-all-done.4 = bf16[4,8,72,1024]{3,2,1,0:T(8,128)(2,1)} async-done(((bf16[4,8,72,1024]{3,2,1,0:T(8,128)(2,1)}), bf16[4,8,72,1024]{3,2,1,0:T(8,128)(2,1)}, u32[]{:S(2)}, u32[]{:S(2)}) %all-to-all-start.4) | async-done | bytes 4718624 | tf_op jit(solution)/shard_map/all_to_all | solution.py:192
  1960.5 57.0 %all-to-all-done.5 = bf16[8,4,72,1024]{3,2,0,1:T(8,128)(2,1)} async-done(((bf16[8,4,72,1024]{3,2,0,1:T(8,128)(2,1)}), bf16[8,4,72,1024]{3,2,0,1:T(8,128)(2,1)}, u32[]{:S(2)}, u32[]{:S(2)}) %all-to-all-start.5) | async-done | bytes 4718624 | tf_op jit(solution)/shard_map/all_to_all | solution.py:206
  2065.3 55.2 %all-reduce.25.cloned.1.call-done = (f32[256,1024]{1,0:T(8,128)}, f32[256,1024]{1,0:T(8,128)}) async-done(((f32[256,1024]{1,0:T(8,128)}, f32[256,1024]{1,0:T(8,128)}), (f32[256,1024]{1,0:T(8,128)}, f32[256,1024]{1,0:T(8,128)})) %all-reduce.25.cloned.1.call-update) | async-done | bytes 2097168 | tf_op jit(solution)/shard_map/psum | solution.py:271
  (1271 shorter events, 1094.9 us)
Async XLA Ops:
  7.2 153.5 %all-reduce.19.cloned.1.call-start = ((), (), s32[]{:S(2)}) async-start(), calls=%async_computation.18 | async-start | bytes 2097152 | tf_op jit(solution)/shard_map/psum | solution.py:252
  251.2 59.2 %all-to-all-start.1 = ((bf16[8,4,72,1024]{3,2,0,1:T(8,128)(2,1)}), bf16[8,4,72,1024]{3,2,0,1:T(8,128)(2,1)}, u32[]{:S(2)}, u32[]{:S(2)}) async-start(bf16[8,4,72,1024]{3,2,0,1:T(8,128)(2,1)} %copy.367), calls=%async_computation.1 | async-start | bytes 9437184 | tf_op jit(solution)/shard_map/all_to_all | solution.py:206
  256.5 124.6 %all-reduce.21.cloned.1.call-start = ((), (), s32[]{:S(2)}) async-start(), calls=%async_computation.19 | async-start | bytes 2097152 | tf_op jit(solution)/shard_map/psum | solution.py:271
  328.9 182.1 %all-reduce.35.cloned.1.call-start = ((), (), s32[]{:S(2)}) async-start(), calls=%async_computation.26 | async-start | bytes 4194304 | tf_op jit(solution)/shard_map/psum | solution.py:252
  594.6 58.8 %all-to-all-start.7 = ((bf16[4,8,72,1024]{3,2,1,0:T(8,128)(2,1)}), bf16[4,8,72,1024]{3,2,1,0:T(8,128)(2,1)}, u32[]{:S(2)}, u32[]{:S(2)}) async-start(bf16[4,8,72,1024]{3,2,1,0:T(8,128)(2,1)} %broadcast_select_fusion.2), calls=%async_computation.7 | async-start | bytes 9437184 | tf_op jit(solution)/shard_map/all_to_all | solution.py:192
  653.5 59.1 %all-to-all-start.2 = ((bf16[4,8,72,1024]{3,2,1,0:T(8,128)(2,1)}), bf16[4,8,72,1024]{3,2,1,0:T(8,128)(2,1)}, u32[]{:S(2)}, u32[]{:S(2)}) async-start(bf16[4,8,72,1024]{3,2,1,0:T(8,128)(2,1)} %broadcast_select_fusion.4), calls=%async_computation.2 | async-start | bytes 9437184 | tf_op jit(solution)/shard_map/all_to_all | solution.py:192
  712.5 59.0 %all-to-all-start.8 = ((bf16[8,4,72,1024]{3,2,0,1:T(8,128)(2,1)}), bf16[8,4,72,1024]{3,2,0,1:T(8,128)(2,1)}, u32[]{:S(2)}, u32[]{:S(2)}) async-start(bf16[8,4,72,1024]{3,2,0,1:T(8,128)(2,1)} %copy.400), calls=%async_computation.8 | async-start | bytes 9437184 | tf_op jit(solution)/shard_map/all_to_all | solution.py:206
  771.5 58.9 %all-to-all-start.3 = ((bf16[8,4,72,1024]{3,2,0,1:T(8,128)(2,1)}), bf16[8,4,72,1024]{3,2,0,1:T(8,128)(2,1)}, u32[]{:S(2)}, u32[]{:S(2)}) async-start(bf16[8,4,72,1024]{3,2,0,1:T(8,128)(2,1)} %copy.377), calls=%async_computation.3 | async-start | bytes 9437184 | tf_op jit(solution)/shard_map/all_to_all | solution.py:206
  830.4 58.8 %all-to-all-start.9 = ((bf16[8,4,72,1024]{3,2,0,1:T(8,128)(2,1)}), bf16[8,4,72,1024]{3,2,0,1:T(8,128)(2,1)}, u32[]{:S(2)}, u32[]{:S(2)}) async-start(bf16[8,4,72,1024]{3,2,0,1:T(8,128)(2,1)} %copy.401), calls=%async_computation.9 | async-start | bytes 9437184 | tf_op jit(solution)/shard_map/all_to_all | solution.py:206
  835.4 127.2 %all-reduce.33.cloned.1.call-start = ((), (), s32[]{:S(2)}) async-start(), calls=%async_computation.25 | async-start | bytes 4194304 | tf_op jit(solution)/shard_map/psum | solution.py:271
  875.4 206.1 %all-reduce.31.cloned.1.call-start = ((), (), s32[]{:S(2)}) async-start(), calls=%async_computation.24 | async-start | bytes 4194304 | tf_op jit(solution)/shard_map/psum | solution.py:252
  1113.0 58.9 %all-to-all-start.11 = ((bf16[4,8,72,1024]{3,2,1,0:T(8,128)(2,1)}), bf16[4,8,72,1024]{3,2,1,0:T(8,128)(2,1)}, u32[]{:S(2)}, u32[]{:S(2)}) async-start(bf16[4,8,72,1024]{3,2,1,0:T(8,128)(2,1)} %broadcast_select_fusion.1), calls=%async_computation.11 | async-start | bytes 9437184 | tf_op jit(solution)/shard_map/all_to_all | solution.py:192
  1171.9 59.1 %all-to-all-start.10 = ((bf16[4,8,72,1024]{3,2,1,0:T(8,128)(2,1)}), bf16[4,8,72,1024]{3,2,1,0:T(8,128)(2,1)}, u32[]{:S(2)}, u32[]{:S(2)}) async-start(bf16[4,8,72,1024]{3,2,1,0:T(8,128)(2,1)} %multiply_convert_fusion.1), calls=%async_computation.10 | async-start | bytes 9437184 | tf_op jit(solution)/shard_map/all_to_all | solution.py:192
  1246.0 58.9 %all-to-all-start.12 = ((bf16[8,4,72,1024]{3,2,0,1:T(8,128)(2,1)}), bf16[8,4,72,1024]{3,2,0,1:T(8,128)(2,1)}, u32[]{:S(2)}, u32[]{:S(2)}) async-start(bf16[8,4,72,1024]{3,2,0,1:T(8,128)(2,1)} %copy.415), calls=%async_computation.12 | async-start | bytes 9437184 | tf_op jit(solution)/shard_map/all_to_all | solution.py:206
  1304.9 58.8 %all-to-all-start.13 = ((bf16[8,4,72,1024]{3,2,0,1:T(8,128)(2,1)}), bf16[8,4,72,1024]{3,2,0,1:T(8,128)(2,1)}, u32[]{:S(2)}, u32[]{:S(2)}) async-start(bf16[8,4,72,1024]{3,2,0,1:T(8,128)(2,1)} %copy.416), calls=%async_computation.13 | async-start | bytes 9437184 | tf_op jit(solution)/shard_map/all_to_all | solution.py:206
  1309.9 88.2 %all-reduce.23.cloned.1.call-start = ((), (), s32[]{:S(2)}) async-start(), calls=%async_computation.20 | async-start | bytes 2097152 | tf_op jit(solution)/shard_map/psum | solution.py:353
  1340.0 152.5 %all-reduce.29.cloned.1.call-start = ((), (), s32[]{:S(2)}) async-start(), calls=%async_computation.23 | async-start | bytes 4194304 | tf_op jit(solution)/shard_map/psum | solution.py:411
  1522.0 59.0 %all-to-all-start.15 = ((bf16[4,8,72,1024]{3,2,1,0:T(8,128)(2,1)}), bf16[4,8,72,1024]{3,2,1,0:T(8,128)(2,1)}, u32[]{:S(2)}, u32[]{:S(2)}) async-start(bf16[4,8,72,1024]{3,2,1,0:T(8,128)(2,1)} %broadcast_select_fusion), calls=%async_computation.15 | async-start | bytes 9437184 | tf_op jit(solution)/shard_map/all_to_all | solution.py:192
  1581.0 58.8 %all-to-all-start.14 = ((bf16[4,8,72,1024]{3,2,1,0:T(8,128)(2,1)}), bf16[4,8,72,1024]{3,2,1,0:T(8,128)(2,1)}, u32[]{:S(2)}, u32[]{:S(2)}) async-start(bf16[4,8,72,1024]{3,2,1,0:T(8,128)(2,1)} %multiply_convert_fusion), calls=%async_computation.14 | async-start | bytes 9437184 | tf_op jit(solution)/shard_map/all_to_all | solution.py:192
  1655.4 59.4 %all-to-all-start.16 = ((bf16[8,4,72,1024]{3,2,0,1:T(8,128)(2,1)}), bf16[8,4,72,1024]{3,2,0,1:T(8,128)(2,1)}, u32[]{:S(2)}, u32[]{:S(2)}) async-start(bf16[8,4,72,1024]{3,2,0,1:T(8,128)(2,1)} %copy.431), calls=%async_computation.16 | async-start | bytes 9437184 | tf_op jit(solution)/shard_map/all_to_all | solution.py:206
  1719.8 118.3 %all-reduce.27.cloned.1.call-start = ((), (), s32[]{:S(2)}) async-start(), calls=%async_computation.22 | async-start | bytes 4194304 | tf_op jit(solution)/shard_map/psum | solution.py:252
  1936.3 81.1 %all-to-all-start.5 = ((bf16[8,4,72,1024]{3,2,0,1:T(8,128)(2,1)}), bf16[8,4,72,1024]{3,2,0,1:T(8,128)(2,1)}, u32[]{:S(2)}, u32[]{:S(2)}) async-start(bf16[8,4,72,1024]{3,2,0,1:T(8,128)(2,1)} %copy.387), calls=%async_computation.5 | async-start | bytes 9437184 | tf_op jit(solution)/shard_map/all_to_all | solution.py:206
  1941.4 115.3 %all-reduce.37.cloned.1.call-start = ((), (), s32[]{:S(2)}) async-start(), calls=%async_computation.27 | async-start | bytes 3276800 | tf_op jit(solution)/shard_map/psum | solution.py:496
  1956.4 164.1 %all-reduce.25.cloned.1.call-start = ((), (), s32[]{:S(2)}) async-start(), calls=%async_computation.21 | async-start | bytes 4194304 | tf_op jit(solution)/shard_map/psum | solution.py:271
  (324 other events, 5757.3 us)
Sparse Core Ops, SparseCore 0:
  41.5 54.5 all-reduce.18
  329.0 52.0 all-reduce.20
  423.6 87.3 all-reduce.34
  875.5 87.0 all-reduce.32
  994.2 87.2 all-reduce.30
  1340.2 51.9 all-reduce.22
  1407.7 84.7 all-reduce.28
  1751.6 86.4 all-reduce.26
  1956.5 65.9 all-reduce.36
  2036.1 84.3 all-reduce.24
where the time goes:
time: 2150 us; the launch traced here: 2140 us
  waiting for transfers between devices  1020 us (47%)
  local copies, waits for them, and re-layouts  416 us (19%)
  other arithmetic  259 us (12%)
  matrix products  231 us (11%)
  starting transfers between devices  97.5 us (5%)
  blocking collectives  96.1 us (4%)
    all_to_all x9, waiting for transfers between devices, from_experts(): lax.all_to_all(expert_out.reshape(local_count, rank_count, slot_count, ex...  309 us
    all_to_all x8, waiting for transfers between devices, to_experts(): lax.all_to_all(slot_rows.reshape(rank_count, local_count, slot_rows.shape...  262 us
    psum x4, waiting for transfers between devices, layer_forward(): lax.psum(jnp.dot(attended, w_o, preferred_element_type=jnp.float32), 'ten...  180 us
    psum x3, waiting for transfers between devices, layer_forward(): lax.psum(jnp.einsum('rk,rkd->rd', gates, picked, preferred_element_type=j...  149 us
    unnamed x642, local copies, waits for them, and re-layouts  80.9 us
    psum x1, waiting for transfers between devices, layer_backward(): grad_normed_in = lax.psum(grad_normed_part, 'tensor')  76.4 us
    another operation x24, other arithmetic  61.2 us
    all_to_all x1, blocking collectives, to_experts(): lax.all_to_all(slot_rows.reshape(rank_count, local_count, slot_rows.shape...  57.8 us
  transfers between devices with their start and end apart: 31, of which 28 were waited for; matrix products, arithmetic and copies ran while one was open for 28% of the time, Pallas kernels for 0%

commit v1 on v0

v1 whole, which is shorter than its diff:
```python
import functools

import jax
import jax.numpy as jnp
from jax import lax
from jax.experimental import pallas as pl
from jax.experimental.pallas import tpu as pltpu
from jax.sharding import PartitionSpec as P

QUERY_HEADS = 16
KEY_VALUE_HEADS = 8
HEAD_SIZE = 64
NE = 32
SLOTS = 4
LANES = 128

EPSILON = 1e-06
THETA_BASE = 10000.0
MASKED = -1e30
TILE = 256
GROUPS = QUERY_HEADS // KEY_VALUE_HEADS
SCORE_SCALE = HEAD_SIZE ** (-0.5)
VMEM_LIMIT = 60 * 1024 * 1024

f32 = jnp.float32
bf16 = jnp.bfloat16


def dot_nn(a, b):
    return lax.dot_general(a, b, (((1,), (0,)), ((), ())), preferred_element_type=f32)


def dot_nt(a, b):
    return lax.dot_general(a, b, (((1,), (1,)), ((), ())), preferred_element_type=f32)


def dot_tn(a, b):
    return lax.dot_general(a, b, (((0,), (0,)), ((), ())), preferred_element_type=f32)


def swap(x, axis, k):
    return lax.ppermute(x, axis, [(i, i ^ k) for i in range(lax.axis_size(axis))])


def shifted(x, by):
    length = lax.axis_size("section")
    return lax.ppermute(x, "section", [(i, i + by) for i in range(length) if 0 <= i + by < length])


def expert_bits():
    n = lax.axis_size("expert")
    bits = []
    k = n // 2
    while k >= 1:
        bits.append(k)
        k //= 2
    return bits


def pieces_tensor(x):
    return [x] + [swap(x, "tensor", k) for k in range(1, lax.axis_size("tensor"))]


def gather_expert(x):
    for k in expert_bits():
        x = jnp.concatenate([x, swap(x, "expert", k)], axis=0)
    return x


def gather_rows(shard):
    low = jnp.concatenate(pieces_tensor(shard), axis=0)
    bits = expert_bits()
    for k in bits[:-1]:
        low = jnp.concatenate([low, swap(low, "expert", k)], axis=0)
    return (low, swap(low, "expert", bits[-1]))


def reduce_rows(low, high):
    bits = list(reversed(expert_bits()))
    for k in bits[:-1]:
        got = swap(high, "expert", k)
        half = low.shape[0] // 2
        high = (low[half:].astype(f32) + got[half:].astype(f32)).astype(bf16)
        low = (low[:half].astype(f32) + got[:half].astype(f32)).astype(bf16)
    got = swap(high, "expert", bits[-1])
    n = lax.axis_size("tensor")
    part = low.shape[0] // n
    cut = [slice(k * part, (k + 1) * part) for k in range(n)]
    total = low[cut[0]].astype(f32) + got[cut[0]].astype(f32)
    sent = [
        swap((low[cut[k]].astype(f32) + got[cut[k]].astype(f32)).astype(bf16), "tensor", k)
        for k in range(1, n)
    ]
    for piece in sent:
        total = total + piece.astype(f32)
    return total


def reduce_pieces(pieces):
    total = pieces[0].astype(f32)
    for k in range(1, len(pieces)):
        total = total + swap(pieces[k], "tensor", k).astype(f32)
    return total


def sum_expert(y):
    bits = list(reversed(expert_bits()))
    for k in bits:
        half = y.shape[0] // 2
        low = (lax.axis_index("expert") & k) == 0
        mine = jnp.where(low, y[:half], y[half:])
        other = jnp.where(low, y[half:], y[:half])
        y = (mine.astype(f32) + swap(other, "expert", k).astype(f32)).astype(y.dtype)
    for k in reversed(bits):
        low = (lax.axis_index("expert") & k) == 0
        theirs = swap(y, "expert", k)
        y = jnp.concatenate([jnp.where(low, y, theirs), jnp.where(low, theirs, y)], axis=0)
    return y


def sum_all_small(y):
    n = lax.axis_size("tensor")
    y = y + sum(swap(y, "tensor", k) for k in range(1, n))
    for k in expert_bits():
        y = y + swap(y, "expert", k)
    return y


def relative(x, axis, index, count):
    shape = x.shape
    k = count // 2
    while k >= 1:
        outer = count // (2 * k)
        inner = shape[axis] // (outer * 2)
        view = x.reshape(shape[:axis] + (outer, 2, inner) + shape[axis + 1 :])
        flipped = jnp.flip(view, axis=axis + 1)
        x = jnp.where((index & k) != 0, flipped, view).reshape(shape)
        k //= 2
    return x


def rope(v, cosine, sine):
    lane = lax.broadcasted_iota(jnp.int32, v.shape, 1) % HEAD_SIZE
    width = v.shape[1]
    left = pltpu.roll(v, width - HEAD_SIZE // 2, 1)
    right = pltpu.roll(v, HEAD_SIZE // 2, 1)
    return v * cosine + jnp.where(lane < HEAD_SIZE // 2, left, right) * sine


def rope_t(g, cosine, sine):
    return rope(g, cosine, -sine)


def twice(v, upper):
    lane = lax.broadcasted_iota(jnp.int32, v.shape, 1)
    keep = lane >= HEAD_SIZE if upper else lane < HEAD_SIZE
    return jnp.where(keep, v, pltpu.roll(v, HEAD_SIZE, 1))


def halves(v):
    lane = lax.broadcasted_iota(jnp.int32, v.shape, 1)
    return (jnp.where(lane < HEAD_SIZE, v, 0.0), jnp.where(lane >= HEAD_SIZE, v, 0.0))


def both(low, high):
    lane = lax.broadcasted_iota(jnp.int32, low.shape, 1)
    return jnp.where(lane < HEAD_SIZE, low, high)


def attn_forward_kernel(count, *refs):
    x_refs = refs[1 : 1 + count]
    gain_ref, wqkv_ref, wo_ref, cos_ref, sin_ref, mask_ref = refs[1 + count : 7 + count]
    part_refs = refs[7 + count : 7 + 2 * count]
    qkv_ref, mixed_ref, normed_ref = refs[7 + 2 * count :]
    x = jnp.concatenate([r[...] for r in x_refs], axis=0).astype(f32)
    scale = lax.rsqrt(jnp.mean(x * x, axis=-1, keepdims=True) + EPSILON)
    normed = (x * scale * gain_ref[...]).astype(bf16)
    normed_ref[...] = normed
    qkv = dot_nn(normed, wqkv_ref[...])
    cosine, sine = cos_ref[...], sin_ref[...]
    q_width = wo_ref.shape[0]
    kv_width = (qkv.shape[1] - q_width) // 2
    groups = []
    for at in range(0, qkv.shape[1], 128):
        piece = qkv[:, at : at + 128]
        if at < q_width + kv_width:
            piece = rope(piece, cosine, sine)
        piece = piece.astype(bf16)
        qkv_ref[:, at : at + 128] = piece
        groups.append(piece.astype(f32))
    allowed = mask_ref[...] > 0.0
    mixed = []
    for g in range(kv_width // HEAD_SIZE):
        k = twice(groups[q_width // 128 + g // 2], g % 2).astype(bf16)
        v = twice(groups[(q_width + kv_width) // 128 + g // 2], g % 2).astype(bf16)
        outs = []
        for q in halves(groups[g]):
            s = jnp.where(allowed, dot_nt(q.astype(bf16), k) * SCORE_SCALE, MASKED)
            p = jnp.exp(s - jnp.max(s, axis=-1, keepdims=True))
            p = (p / jnp.sum(p, axis=-1, keepdims=True)).astype(bf16)
            outs.append(dot_nn(p, v))
        mixed.append(both(*outs).astype(bf16))
    mixed = jnp.concatenate(mixed, axis=1)
    mixed_ref[...] = mixed
    part = dot_nn(mixed, wo_ref[...]).astype(bf16)
    rows = part.shape[0] // count
    for j in range(count):
        part_refs[j][...] = part[j * rows : (j + 1) * rows]


def attn_backward_kernel(count, *refs):
    gm_refs = refs[1 : 1 + count]
    x_refs = refs[1 + count : 1 + 2 * count]
    qkv_ref, wqkv_ref, wo_ref, cos_ref, sin_ref, mask_ref = refs[1 + 2 * count : 7 + 2 * count]
    part_refs = refs[7 + 2 * count : 7 + 3 * count]
    gqkv_ref, gain_ref, gm_ref = refs[7 + 3 * count :]
    gm = jnp.concatenate([r[...] for r in gm_refs], axis=0)
    gm_ref[...] = gm
    cosine, sine = cos_ref[...], sin_ref[...]
    q_width = wo_ref.shape[0]
    kv_width = (qkv_ref.shape[1] - q_width) // 2
    gmix = dot_nt(gm, wo_ref[...]).astype(bf16).astype(f32)
    allowed = mask_ref[...] > 0.0
    grads = [None] * (qkv_ref.shape[1] // 128)
    for g in range(kv_width // HEAD_SIZE):
        k_at = q_width // 128 + g // 2
        v_at = (q_width + kv_width) // 128 + g // 2
        k = twice(qkv_ref[:, k_at * 128 : k_at * 128 + 128].astype(f32), g % 2).astype(bf16)
        v = twice(qkv_ref[:, v_at * 128 : v_at * 128 + 128].astype(f32), g % 2).astype(bf16)
        qs = halves(qkv_ref[:, g * 128 : g * 128 + 128].astype(f32))
        gxs = halves(gmix[:, g * 128 : g * 128 + 128])
        gqs, gk, gv = [], None, None
        for q, gx in zip(qs, gxs):
            q, gx = q.astype(bf16), gx.astype(bf16)
            s = jnp.where(allowed, dot_nt(q, k) * SCORE_SCALE, MASKED)
            p = jnp.exp(s - jnp.max(s, axis=-1, keepdims=True))
            p = p / jnp.sum(p, axis=-1, keepdims=True)
            gp = dot_nt(gx, v)
            gs = p * (gp - jnp.sum(p * gp, axis=-1, keepdims=True))
            gqs.append(dot_nn(gs.astype(bf16), k) * SCORE_SCALE)
            gk_h = dot_nn(gs.T.astype(bf16), q)
            gv_h = dot_nn(p.T.astype(bf16), gx)
            gk = gk_h if gk is None else gk + gk_h
            gv = gv_h if gv is None else gv + gv_h
        grads[g] = both(*gqs)
        gk = (gk + pltpu.roll(gk, HEAD_SIZE, 1)) * SCORE_SCALE
        gv = gv + pltpu.roll(gv, HEAD_SIZE, 1)
        grads[k_at] = gk if g % 2 == 0 else both(grads[k_at], gk)
        grads[v_at] = gv if g % 2 == 0 else both(grads[v_at], gv)
    for j in range(len(grads)):
        piece = grads[j]
        if j * 128 < q_width + kv_width:
            piece = rope_t(piece, cosine, sine)
        grads[j] = piece.astype(bf16)
    gqkv = jnp.concatenate(grads, axis=1)
    gqkv_ref[...] = gqkv
    part = dot_nt(gqkv, wqkv_ref[...])
    rows = part.shape[0] // count
    for j in range(count):
        part_refs[j][...] = part[j * rows : (j + 1) * rows].astype(bf16)
    x = jnp.concatenate([r[...] for r in x_refs], axis=0).astype(f32)
    scale = lax.rsqrt(jnp.mean(x * x, axis=-1, keepdims=True) + EPSILON)
    gain_ref[...] = jnp.sum(part * x * scale, axis=0, keepdims=True)


def pick_half(low_ref, high_ref, steps):
    return jnp.where(pl.program_id(0) < steps // 2, high_ref[...], low_ref[...])


def put_half(low_ref, high_ref, steps, value):
    @pl.when(pl.program_id(0) < steps // 2)
    def _():
        high_ref[...] = value

    @pl.when(pl.program_id(0) >= steps // 2)
    def _():
        low_ref[...] = value


def expert_forward_kernel(
    steps, dep_ref, xl_ref, xh_ref, sel_ref, wr_ref, wcat_ref, wd_ref, low_ref, high_ref, probs_ref
):
    x = pick_half(xl_ref, xh_ref, steps)
    sel = sel_ref[...]
    width = wd_ref.shape[0]
    count = width // 128
    logits = jnp.where(sel > 0.0, dot_nn(x, wr_ref[...]), MASKED)
    probs = jnp.exp(logits - jnp.max(logits, axis=-1, keepdims=True)) * sel
    probs = probs / jnp.maximum(jnp.sum(probs, axis=-1, keepdims=True), 1e-30)
    probs_ref[...] = probs
    hidden = []
    for e in range(count):
        h = dot_nn(x, wcat_ref[:, e * 256 : (e + 1) * 256])
        gate, up = h[:, :128], h[:, 128:]
        hidden.append((gate * jax.nn.sigmoid(gate) * up * probs[:, e : e + 1]).astype(bf16))
    out = dot_nn(jnp.concatenate(hidden, axis=1), wd_ref[...]).astype(bf16)
    put_half(low_ref, high_ref, steps, out)


def expert_backward_kernel(
    steps, dep_ref, xl_ref, xh_ref, gl_ref, gh_ref, sel_ref, wr_ref, wcat_ref, wd_ref,
    low_ref, high_ref, act_ref, hid_ref, glog_ref,
):
    x = pick_half(xl_ref, xh_ref, steps)
    gy = pick_half(gl_ref, gh_ref, steps)
    sel = sel_ref[...]
    width = wd_ref.shape[0]
    count = width // 128
    logits = jnp.where(sel > 0.0, dot_nn(x, wr_ref[...]), MASKED)
    probs = jnp.exp(logits - jnp.max(logits, axis=-1, keepdims=True)) * sel
    probs = probs / jnp.maximum(jnp.sum(probs, axis=-1, keepdims=True), 1e-30)
    lane = lax.broadcasted_iota(jnp.int32, probs.shape, 1)
    grad_act = dot_nt(gy, wd_ref[...])
    grad_gates = jnp.zeros(probs.shape, f32)
    pieces = []
    for e in range(count):
        h = dot_nn(x, wcat_ref[:, e * 256 : (e + 1) * 256])
        gate, up = h[:, :128], h[:, 128:]
        s = jax.nn.sigmoid(gate)
        silu = gate * s
        hid = silu * up
        ga = grad_act[:, e * 128 : (e + 1) * 128]
        p = probs[:, e : e + 1]
        grad_gates = jnp.where(
            lane == e, jnp.sum(hid * ga, axis=-1, keepdims=True), grad_gates
        )
        gp = ga * p
        pieces.append((gp * up * s * (1.0 + gate * (1.0 - s))).astype(bf16))
        pieces.append((gp * silu).astype(bf16))
        hid_ref[:, e * 128 : (e + 1) * 128] = (hid * p).astype(bf16)
    gcat = jnp.concatenate(pieces, axis=1)
    act_ref[...] = gcat
    glog = probs * (grad_gates - jnp.sum(probs * grad_gates, axis=-1, keepdims=True))
    glog = glog.astype(bf16)
    glog_ref[...] = glog
    out = (dot_nt(gcat, wcat_ref[...]) + dot_nt(glog, wr_ref[...])).astype(bf16)
    put_half(low_ref, high_ref, steps, out)


def expert_weights_kernel(count, micro_count, *refs):
    xt_refs = refs[1 : 1 + count]
    gy_refs = refs[1 + count : 1 + 2 * count]
    act_refs = refs[1 + 2 * count : 1 + 2 * count + micro_count]
    hid_refs = refs[1 + 2 * count + micro_count : 1 + 2 * count + 2 * micro_count]
    gate_ref, up_ref, down_ref = refs[1 + 2 * count + 2 * micro_count :]
    rows = gy_refs[0].shape[0]
    per = count // micro_count
    for at in range(0, xt_refs[0].shape[0], 256):
        grads = sum(
            dot_nn(
                xt_refs[j][at : at + 256, :],
                act_refs[j // per][(j % per) * rows : (j % per + 1) * rows, :],
            )
            for j in range(count)
        )
        for j in range(grads.shape[1] // 256):
            gate_ref[j, at : at + 256, :] = grads[:, j * 256 : j * 256 + 128]
            up_ref[j, at : at + 256, :] = grads[:, j * 256 + 128 : j * 256 + 256]
    down = sum(
        dot_nn(hid_refs[j // per][:, (j % per) * rows : (j % per + 1) * rows], gy_refs[j][...])
        for j in range(count)
    )
    for j in range(down.shape[0] // 128):
        down_ref[j] = down[j * 128 : (j + 1) * 128, :]


def full(array):
    zeros = (0,) * array.ndim
    return pl.BlockSpec(array.shape, lambda *_: zeros)


def once(array):
    zeros = (0,) * array.ndim
    return pl.BlockSpec(array.shape, lambda *_: zeros, pipeline_mode=pl.Buffered(1))


ANYWHERE = pl.BlockSpec(memory_space=pl.ANY)


def params():
    return pltpu.CompilerParams(vmem_limit_bytes=VMEM_LIMIT)


def cost(flops, moved):
    return pl.CostEstimate(flops=int(flops), bytes_accessed=int(moved), transcendentals=0)


def attn_forward(dep, xs, gain, wqkv, wo, cosine, sine, mask):
    count = len(xs)
    part, width = xs[0].shape
    rows = part * count
    heads = wqkv.shape[1]
    args = (*xs, gain, wqkv, wo, cosine, sine, mask)
    outs = (jax.ShapeDtypeStruct((part, width), bf16),) * count + (
        jax.ShapeDtypeStruct((rows, heads), bf16),
        jax.ShapeDtypeStruct((rows, wo.shape[0]), bf16),
        jax.ShapeDtypeStruct((rows, width), bf16),
    )
    out = pl.pallas_call(
        functools.partial(attn_forward_kernel, count),
        out_shape=outs,
        in_specs=[ANYWHERE] + [full(a) for a in args],
        out_specs=[full(o) for o in outs],
        compiler_params=params(),
        cost_estimate=cost(2 * rows * width * (heads + wo.shape[0]), 4e6),
        name="attn_forward",
    )(dep, *args)
    return (out[:count], *out[count:])


def attn_backward(dep, gms, xs, qkv, wqkv, wo, cosine, sine, mask):
    count = len(xs)
    part, width = xs[0].shape
    rows = part * count
    heads = wqkv.shape[1]
    args = (*gms, *xs, qkv, wqkv, wo, cosine, sine, mask)
    outs = (jax.ShapeDtypeStruct((part, width), bf16),) * count + (
        jax.ShapeDtypeStruct((rows, heads), bf16),
        jax.ShapeDtypeStruct((1, width), f32),
        jax.ShapeDtypeStruct((rows, width), bf16),
    )
    out = pl.pallas_call(
        functools.partial(attn_backward_kernel, count),
        out_shape=outs,
        in_specs=[ANYWHERE] + [full(a) for a in args],
        out_specs=[full(o) for o in outs],
        compiler_params=params(),
        cost_estimate=cost(2 * rows * width * (heads + wo.shape[0]), 4e6),
        name="attn_backward",
    )(dep, *args)
    return (out[:count], *out[count:])


def half_specs(rows, width):
    half = rows // (2 * TILE)
    low = pl.BlockSpec((TILE, width), lambda i: (jnp.maximum(i - half, 0), 0))
    high = pl.BlockSpec((TILE, width), lambda i: (jnp.minimum(i, half - 1), 0))
    whole = lambda w: pl.BlockSpec((TILE, w), lambda i: ((i + half) % (2 * half), 0))
    return (low, high, whole)


def expert_forward(dep, x, sel, wr, wcat, wd):
    half, width = x[0].shape
    rows = 2 * half
    low, high, whole = half_specs(rows, width)
    outs = (
        jax.ShapeDtypeStruct((half, width), bf16),
        jax.ShapeDtypeStruct((half, width), bf16),
        jax.ShapeDtypeStruct((rows, LANES), f32),
    )
    return pl.pallas_call(
        functools.partial(expert_forward_kernel, rows // TILE),
        out_shape=outs,
        grid=(rows // TILE,),
        in_specs=[ANYWHERE, low, high, whole(LANES), once(wr), once(wcat), once(wd)],
        out_specs=[low, high, whole(LANES)],
        compiler_params=params(),
        cost_estimate=cost(2 * rows * 3 * wcat.size / 2, 12e6),
        name="expert_forward",
    )(dep, *x, sel, wr, wcat, wd)


def expert_backward(dep, x, gy, sel, wr, wcat, wd):
    half, width = x[0].shape
    rows = 2 * half
    low, high, whole = half_specs(rows, width)
    outs = (
        jax.ShapeDtypeStruct((half, width), bf16),
        jax.ShapeDtypeStruct((half, width), bf16),
        jax.ShapeDtypeStruct((rows, wcat.shape[1]), bf16),
        jax.ShapeDtypeStruct((rows, wd.shape[0]), bf16),
        jax.ShapeDtypeStruct((rows, LANES), bf16),
    )
    return pl.pallas_call(
        functools.partial(expert_backward_kernel, rows // TILE),
        out_shape=outs,
        grid=(rows // TILE,),
        in_specs=[ANYWHERE, low, high, low, high, whole(LANES), once(wr), once(wcat), once(wd)],
        out_specs=[low, high, whole(wcat.shape[1]), whole(wd.shape[0]), whole(LANES)],
        compiler_params=params(),
        cost_estimate=cost(2 * rows * 5 * wcat.size / 2, 20e6),
        name="expert_backward",
    )(dep, *x, *gy, sel, wr, wcat, wd)


def expert_weights(dep, xts, gys, acts, hids):
    micro_count = len(acts)
    count = len(xts)
    width, half = xts[0].shape
    rows = acts[0].shape[0]
    local = hids[0].shape[0] // 128
    pair = 2 if rows <= 1024 else 1
    outs = (
        jax.ShapeDtypeStruct((local, width, 128), f32),
        jax.ShapeDtypeStruct((local, width, 128), f32),
        jax.ShapeDtypeStruct((local, 128, width), f32),
    )
    return pl.pallas_call(
        functools.partial(expert_weights_kernel, count, micro_count),
        out_shape=outs,
        grid=(local // pair,),
        in_specs=[ANYWHERE]
        + [once(a) for a in xts]
        + [once(a) for a in gys]
        + [pl.BlockSpec((rows, 256 * pair), lambda i: (0, i))] * micro_count
        + [pl.BlockSpec((128 * pair, rows), lambda i: (i, 0))] * micro_count,
        out_specs=[
            pl.BlockSpec((pair, width, 128), lambda i: (i, 0, 0)),
            pl.BlockSpec((pair, width, 128), lambda i: (i, 0, 0)),
            pl.BlockSpec((pair, 128, width), lambda i: (i, 0, 0)),
        ],
        compiler_params=params(),
        cost_estimate=cost(2 * micro_count * rows * width * 3 * 128 * local, 36e6),
        name="expert_weights",
    )(dep, *xts, *gys, *acts, *hids)


def rms_scale(values):
    return lax.rsqrt(jnp.mean(values * values, axis=-1, keepdims=True) + EPSILON)


def norm_backward(grad_normed, values, scale_rows, gain):
    weighted = grad_normed * gain
    return scale_rows * weighted - values * scale_rows**3 * jnp.mean(
        values * weighted, axis=-1, keepdims=True
    )


def layout(lengths, row_ids):
    seq_ends = jnp.cumsum(lengths)
    starts = jnp.concatenate([seq_ends - lengths, seq_ends[-1:]])
    segment = jnp.sum((row_ids[:, None] >= seq_ends[None, :]).astype(jnp.int32), axis=1)
    picked = segment[:, None] == jnp.arange(SLOTS + 1, dtype=jnp.int32)[None, :]
    begins = jnp.sum(jnp.where(picked, starts[None, :], 0), axis=1)
    return (segment, (row_ids - begins).astype(f32))


def tables(position):
    frequency = THETA_BASE ** (-jnp.arange(0, HEAD_SIZE, 2, dtype=f32) / HEAD_SIZE)
    angles = position[:, None] * frequency[None, :]
    cosine, sine = jnp.cos(angles), jnp.sin(angles)
    cosine = jnp.concatenate([cosine] * 4, axis=-1)
    sine = jnp.concatenate([-sine, sine] * 2, axis=-1)
    return (cosine, sine)


def local(
    inputs,
    cotangent,
    seq_lengths,
    routes,
    gain_attn,
    w_query,
    key_projection,
    value_projection,
    w_out,
    gain_moe,
    w_router,
    w_gate,
    w_up,
    w_down,
):
    first = lax.axis_index("section") == 0
    e_no = lax.axis_index("expert")
    t_no = lax.axis_index("tensor")
    n_t = lax.axis_size("tensor")
    micro_count, rows, width = inputs.shape
    local_experts = w_gate.shape[1]
    micro = range(micro_count)
    part = rows // n_t

    gain_a = gain_attn.astype(f32)
    gain_m = gain_moe.astype(f32)
    wqkv = jnp.concatenate([w_query[0], key_projection[0], value_projection[0]], axis=1)
    wo = w_out[0]
    wr = jnp.pad(jnp.roll(w_router[0], -e_no * local_experts, axis=1), ((0, 0), (0, LANES - NE)))
    wcat = jnp.concatenate(
        [jnp.swapaxes(w_gate[0], 0, 1), jnp.swapaxes(w_up[0], 0, 1)], axis=2
    ).reshape(width, 256 * local_experts)
    wd = w_down[0].reshape(local_experts * 128, width)

    base = jnp.arange(rows, dtype=jnp.int32)
    row_ids = (((base // part) ^ t_no) * part) + base % part
    x_rel = relative(inputs, 1, t_no, n_t)
    routes_rel = relative(routes, 1, t_no, n_t)
    cosines, sines, masks, sels = [], [], [], []
    for m in micro:
        segment, position = layout(seq_lengths[m], row_ids)
        cosine, sine = tables(position)
        cosines.append(cosine)
        sines.append(sine)
        allowed = (segment[:, None] == segment[None, :]) & (row_ids[None, :] <= row_ids[:, None])
        masks.append(allowed.astype(f32))
        named = jnp.where((segment < SLOTS)[:, None], routes_rel[m], -1)
        sels.append(gather_expert(named))
    for m in micro:
        named = sels[m]
        shift = (jnp.arange(NE, dtype=jnp.int32) + e_no * local_experts) % NE
        shift = jnp.where(jnp.arange(LANES) < NE, jnp.pad(shift, (0, LANES - NE)), -2)
        sels[m] = jnp.any(named[:, :, None] == shift[None, None, :], axis=1).astype(f32)

    def attend(m, dep, xs):
        parts, qkv, mixed, normed = attn_forward(
            dep, xs, gain_a, wqkv, wo, cosines[m], sines[m], masks[m]
        )
        middle = xs[0].astype(f32) + reduce_pieces(parts)
        scale_mid = rms_scale(middle)
        normed_mid = (middle * scale_mid * gain_m).astype(bf16)
        return dict(
            xs=xs, qkv=qkv, mixed=mixed, normed=normed, middle=middle, scale_mid=scale_mid,
            rows=gather_rows(normed_mid),
        )

    def finish(saved, out):
        return (saved["middle"] + reduce_rows(out[0], out[1])).astype(bf16)

    def experts(m, dep, saved):
        return expert_forward(dep, saved["rows"], sels[m], wr, wcat, wd)

    def experts_back(m, dep, saved, gathered):
        return expert_backward(dep, saved["rows"], gathered, sels[m], wr, wcat, wd)

    def attend_back(m, dep, saved, grad_y, out):
        grad_normed = reduce_rows(out[0], out[1])
        middle, scale_mid = saved["middle"], saved["scale_mid"]
        g_gain_m = jnp.sum(grad_normed * middle * scale_mid, axis=0, keepdims=True)
        grad_middle = norm_backward(grad_normed, middle, scale_mid, gain_m) + grad_y.astype(f32)
        gms = pieces_tensor(grad_middle.astype(bf16))
        parts, gqkv, g_gain_a, gm = attn_backward(
            dep, gms, saved["xs"], saved["qkv"], wqkv, wo, cosines[m], sines[m], masks[m]
        )
        grad_normed_in = reduce_pieces(parts)
        resid = saved["xs"][0].astype(f32)
        grad_in = norm_backward(grad_normed_in, resid, rms_scale(resid), gain_a) + grad_middle
        return dict(
            gm=gm, gqkv=gqkv, g_gain_m=g_gain_m, g_gain_a=g_gain_a, grad_in=grad_in.astype(bf16)
        )

    def shared_grads(saved, outs, back):
        def total(left, right):
            return sum(dot_tn(saved[m][left], back[m][right]) for m in micro)

        g_router = sum(
            dot_tn(saved[m]["rows"][j], outs[m][4][j * half : (j + 1) * half])
            for m in micro
            for j in range(2)
        )
        return (
            total("normed", "gqkv"),
            total("mixed", "gm"),
            sum(back[m]["g_gain_a"] for m in micro),
            sum(back[m]["g_gain_m"] for m in micro),
            g_router,
        )

    def expert_grads(dep, saved, gathered, outs):
        return expert_weights(
            dep,
            [x.T for s in saved for x in s["rows"]],
            [g for pair in gathered for g in pair],
            [o[2] for o in outs],
            [o[3].T for o in outs],
        )

    half = rows * lax.axis_size("expert") // 2
    x_cut = [[x_rel[m, k * part : (k + 1) * part] for k in range(n_t)] for m in micro]
    cot = [relative(cotangent[m], 0, t_no, n_t)[:part] for m in micro]
    dep = wqkv

    saved0 = []
    for m in micro:
        saved0.append(attend(m, dep, x_cut[m]))
        dep = saved0[m]["qkv"]
    out0 = []
    for m in micro:
        out0.append(experts(m, dep, saved0[m]))
        dep = out0[m][2]
    shard0 = [finish(saved0[m], out0[m]) for m in micro]
    saved1 = []
    for m in micro:
        saved1.append(attend(m, dep, pieces_tensor(shifted(shard0[m], 1))))
        dep = saved1[m]["qkv"]
    gathered1 = [gather_rows(cot[m]) for m in micro]
    back_out1 = []
    for m in micro:
        back_out1.append(experts_back(m, dep, saved1[m], gathered1[m]))
        dep = back_out1[m][4]
    back1 = []
    for m in micro:
        back1.append(attend_back(m, dep, saved1[m], cot[m], back_out1[m]))
        dep = back1[m]["g_gain_a"]
    returned = [shifted(back1[m]["grad_in"], -1) for m in micro]
    experts1 = expert_grads(dep, saved1, gathered1, back_out1)
    dep = experts1[0]
    out1 = [experts(0, dep, saved1[0])]
    dep = out1[0][2]
    gathered0 = [gather_rows(returned[m]) for m in micro]
    back_out0 = []
    for m in micro:
        back_out0.append(experts_back(m, dep, saved0[m], gathered0[m]))
        dep = back_out0[m][4]
    for m in micro[1:]:
        out1.append(experts(m, dep, saved1[m]))
        dep = out1[m][2]
    shard1 = [finish(saved1[m], out1[m]) for m in micro]
    back0 = []
    for m in micro:
        back0.append(attend_back(m, dep, saved0[m], returned[m], back_out0[m]))
        dep = back0[m]["g_gain_a"]
    grads1 = shared_grads(saved1, back_out1, back1)
    grads0 = shared_grads(saved0, back_out0, back0)
    g_gate, g_up, g_down = lax.cond(
        first,
        lambda: tuple(expert_grads(dep, saved0, gathered0, back_out0)),
        lambda: tuple(experts1),
    )

    g_qkv, g_out, g_gain_a, g_gain_m, g_router = (
        jnp.where(first, a, b) for a, b in zip(grads0, grads1)
    )
    g_qkv = sum_expert(g_qkv.astype(bf16)).astype(f32)
    g_out = sum_expert(g_out.astype(bf16)).astype(f32)
    g_gains = sum_all_small(jnp.concatenate([g_gain_a, g_gain_m], axis=0))
    g_router = jnp.roll(g_router[:, :NE], e_no * local_experts, axis=1)
    g_router = lax.psum(g_router, ("expert", "tensor"))

    def assemble(shards):
        whole = [jnp.concatenate(pieces_tensor(s), axis=0) for s in shards]
        return jnp.stack([relative(w, 0, t_no, n_t) for w in whole])[None]

    activations = assemble([jnp.where(first, shard0[m], shard1[m]) for m in micro])
    input_grads = assemble(
        [jnp.where(first, back0[m]["grad_in"], back1[m]["grad_in"]) for m in micro]
    )
    q_width = w_query.shape[2]
    kv_width = key_projection.shape[2]
    return (
        activations,
        input_grads,
        g_gains[:1],
        g_qkv[None, :, :q_width],
        g_qkv[None, :, q_width : q_width + kv_width],
        g_qkv[None, :, q_width + kv_width :],
        g_out[None],
        g_gains[1:],
        g_router[None],
        g_gate[None],
        g_up[None],
        g_down[None],
    )


def solution(mesh):
    in_specs = (
        P(None, "expert", None),
        P(None, "expert", None),
        P(None, "expert"),
        P(None, "expert", None),
        P("section", None),
        P("section", None, "tensor"),
        P("section", None, "tensor"),
        P("section", None, "tensor"),
        P("section", "tensor", None),
        P("section", None),
        P("section", None, None),
        P("section", "expert", None, "tensor"),
        P("section", "expert", None, "tensor"),
        P("section", "expert", "tensor", None),
    )
    out_specs = (
        P("section", None, "expert", None),
        P("section", None, "expert", None),
        P("section", None),
        P("section", None, "tensor"),
        P("section", None, "tensor"),
        P("section", None, "tensor"),
        P("section", "tensor", None),
        P("section", None),
        P("section", None, None),
        P("section", "expert", None, "tensor"),
        P("section", "expert", None, "tensor"),
        P("section", "expert", "tensor", None),
    )
    return jax.shard_map(local, mesh=mesh, in_specs=in_specs, out_specs=out_specs, check_vma=False)
```

time: 2150 us -> 826 us (0.38)
  waiting for transfers between devices: 1020 us -> 210 us
  local copies, waits for them, and re-layouts: 416 us -> 60.2 us
  Pallas kernels: 0 us -> 215 us
  matrix products: 231 us -> 19 us
  other arithmetic: 259 us -> 73.1 us
  starting transfers between devices: 97.5 us -> 222 us
  blocking collectives: 96.1 us -> 0 us
    all_to_all x17 -> x0, waiting for transfers between devices: 571 us -> none  [the longest x9 309 us: from_experts(): lax.all_to_all(expert_out.reshape(local_count, rank_count, slot_count, ex...]
    psum x10 -> x1, waiting for transfers between devices: 406 us -> 0.01 us  [local(): g_router = lax.psum(g_router, ('expert', 'tensor'))]
    gather x24 -> x0, local copies, waits for them, and re-layouts: 237 us -> none  [the longest x6 49.1 us: layer_forward(): normed_mid[source]]
    pallas_call x0 -> x18, Pallas kernels: none -> 215 us  [the longest x4 84.2 us: expert_backward(): pl.pallas_call(functools.partial(expert_backward_kernel, rows // TILE), o...]
    ppermute x4 -> x155, starting transfers between devices: 9.49 us -> 222 us  [the longest x151 212 us: swap(): lax.ppermute(x, axis, [(i, i ^ k) for i in range(lax.axis_size(axis))])]
    dot_general x123 -> x16, matrix products: 225 us -> 19 us  [dot_tn(): lax.dot_general(a, b, (((0,), (0,)), ((), ())), preferred_element_type=f32)]
    ppermute x4 -> x155, waiting for transfers between devices: 46.9 us -> 210 us  [the longest x151 208 us: swap(): lax.ppermute(x, axis, [(i, i ^ k) for i in range(lax.axis_size(axis))])]
    all_to_all x17 -> x0, starting transfers between devices: 86.6 us -> none  [the longest x9 46.1 us: from_experts(): lax.all_to_all(expert_out.reshape(local_count, rank_count, slot_count, ex...]
  transfers between devices with their start and end apart: 31 -> 156, of which waited for: 28 -> 52; matrix products, arithmetic and copies ran while one was open for 28% -> 15% of each run, Pallas kernels for 0% -> 16%
where the time goes in v1:
time: 826 us; the launch traced here: 817 us
  starting transfers between devices  222 us (27%)
  Pallas kernels  215 us (26%)
  waiting for transfers between devices  210 us (25%)
  other arithmetic  73.1 us (9%)
  local copies, waits for them, and re-layouts  60.2 us (7%)
  matrix products  19 us (2%)
  between operations  16.8 us (2%)
    ppermute x151, starting transfers between devices, swap(): lax.ppermute(x, axis, [(i, i ^ k) for i in range(lax.axis_size(axis))])  212 us
    ppermute x151, waiting for transfers between devices, swap(): lax.ppermute(x, axis, [(i, i ^ k) for i in range(lax.axis_size(axis))])  208 us
    pallas_call x4, Pallas kernels, expert_backward(): pl.pallas_call(functools.partial(expert_backward_kernel, rows // TILE), o...  84.2 us
    pallas_call x4, Pallas kernels, expert_forward(): pl.pallas_call(functools.partial(expert_forward_kernel, rows // TILE), ou...  50.9 us
    pallas_call x2, Pallas kernels, expert_weights(): pl.pallas_call(functools.partial(expert_weights_kernel, count, micro_coun...  38.5 us
    pallas_call x4, Pallas kernels, attn_backward(): pl.pallas_call(functools.partial(attn_backward_kernel, count), out_shape=...  23.6 us
    dot_general x16, matrix products, dot_tn(): lax.dot_general(a, b, (((0,), (0,)), ((), ())), preferred_element_type=f32)  19 us
    pallas_call x4, Pallas kernels, attn_forward(): pl.pallas_call(functools.partial(attn_forward_kernel, count), out_shape=o...  17.9 us
  transfers between devices with their start and end apart: 156, of which 52 were waited for; matrix products, arithmetic and copies ran while one was open for 15% of the time, Pallas kernels for 16%

profile of v1, /device:TPU:0, one launch (start us, length us, event | category | flops | bytes accessed | tf_op | source)
XLA Modules:
  0.0 816.7 jit_solution(7548991143902254856)
XLA Ops:
  104.0 12.5 %expert_forward.4 = (bf16[512,1024]{1,0:T(8,128)(2,1)}, bf16[512,1024]{1,0:T(8,128)(2,1)}, f32[1024,128]{1,0:T(8,128)}) custom-call(bf16[256,512]{1,0:T(8,128)(2,1)} %get-tuple-element.169.dep_ref.refs_9_, bf16[512,1024]{1,0:T(8,128)(2,1)S(1)} %constant_dynamic-update-slice_fusion.xl_ref, bf16[512,1024]{1,0:T(8,128)(2,1)} %collective-permute-done.7.xh_ref, ...), custom_call_target="tpu_custom_call" | custom-call | flops 6442450944 | bytes 12000000 | tf_op jit(solution)/shard_map/expert_forward/pallas_call | solution.py:451
  117.0 12.6 %expert_forward.5 = (bf16[512,1024]{1,0:T(8,128)(2,1)}, bf16[512,1024]{1,0:T(8,128)(2,1)}, f32[1024,128]{1,0:T(8,128)}) custom-call(f32[1024,128]{1,0:T(8,128)} %get-tuple-element.172.dep_ref, bf16[512,1024]{1,0:T(8,128)(2,1)S(1)} %constant_dynamic-update-slice_fusion.5.xl_ref, bf16[512,1024]{1,0:T(8,128)(2,1)} %collective-permute-done.23.xh_ref, ...), custom_call_target="tpu_custom_call" | custom-call | flops 6442450944 | bytes 12000000 | tf_op jit(solution)/shard_map/expert_forward/pallas_call | solution.py:451
  135.8 6.9 collective-permute-start.46
  148.8 7.0 collective-permute-start.13
  157.6 6.9 collective-permute-start.12
  188.1 7.4 collective-permute-done.27.refs_3_.refs_7_
  231.6 8.6 %collective-permute-done.52 = bf16[64,1024]{1,0:T(8,128)(2,1)S(1)} collective-permute-done((bf16[64,1024]{1,0:T(8,128)(2,1)}, bf16[64,1024]{1,0:T(8,128)(2,1)S(1)}, u32[]{:S(2)}, u32[]{:S(2)}) %collective-permute-start.52) | collective-permute-done | bytes 131104 | tf_op jit(solution)/shard_map/ppermute | solution.py:42
  278.6 7.8 collective-permute-done.57
  288.6 21.2 %expert_backward.4 = (bf16[512,1024]{1,0:T(8,128)(2,1)}, bf16[512,1024]{1,0:T(8,128)(2,1)}, bf16[1024,2048]{1,0:T(8,128)(2,1)}, bf16[1024,1024]{1,0:T(8,128)(2,1)}, bf16[1024,128]{1,0:T(8,128)(2,1)}) custom-call(bf16[256,512]{1,0:T(8,128)(2,1)} %get-tuple-element.185.dep_ref.refs_9_, bf16[512,1024]{1,0:T(8,128)(2,1)} %copy-done.9, ...), custom_call_target="tpu_custom_call" | custom-call | flops 10737418240 | bytes 20000000 | tf_op jit(solution)/shard_map/expert_backward/pallas_call | solution.py:474
  309.8 21.0 %expert_backward.5 = (bf16[512,1024]{1,0:T(8,128)(2,1)}, bf16[512,1024]{1,0:T(8,128)(2,1)}, bf16[1024,2048]{1,0:T(8,128)(2,1)}, bf16[1024,1024]{1,0:T(8,128)(2,1)}, bf16[1024,128]{1,0:T(8,128)(2,1)}) custom-call(bf16[1024,128]{1,0:T(8,128)(2,1)} %get-tuple-element.186.dep_ref, bf16[512,1024]{1,0:T(8,128)(2,1)} %copy-done.4, ...), custom_call_target="tpu_custom_call" | custom-call | flops 10737418240 | bytes 20000000 | tf_op jit(solution)/shard_map/expert_backward/pallas_call | solution.py:474
  370.9 8.0 collective-permute-done.67
  417.2 19.4 %expert_weights.3 = (f32[8,1024,128]{2,1,0:T(8,128)}, f32[8,1024,128]{2,1,0:T(8,128)}, f32[8,128,1024]{2,1,0:T(8,128)}) custom-call(f32[1,1024]{1,0:T(1,128)} %get-tuple-element.197.refs_0_, bf16[1024,512]{1,0:T(8,128)(2,1)} %copy.83.refs_1_, bf16[1024,512]{1,0:T(8,128)(2,1)} %copy.84.refs_2_, bf16[1024,512]{1,0:T(8,128)(2,1)} %copy.85.refs_3_, ...), custom_call_target="tpu_custom_call" | custom-call | flops 12884901888 | bytes 36000000 | tf_op jit(solution)/shard_map/expert_weights/pallas_call | solution.py:498
  444.1 12.8 %expert_forward.6 = (bf16[512,1024]{1,0:T(8,128)(2,1)}, bf16[512,1024]{1,0:T(8,128)(2,1)}, f32[1024,128]{1,0:T(8,128)}) custom-call(f32[8,1024,128]{2,1,0:T(8,128)} %get-tuple-element.484.dep_ref, bf16[512,1024]{1,0:T(8,128)(2,1)} %copy-done.9, bf16[512,1024]{1,0:T(8,128)(2,1)} %copy-done.14, f32[1024,128]{1,0:T(8,128)} %convert_element_type.761.sel_ref, ...), custom_call_target="tpu_custom_call" | custom-call | flops 6442450944 | bytes 12000000 | tf_op jit(solution)/shard_map/expert_forward/pallas_call | solution.py:451
  496.2 12.5 %collective-permute-done.81 = bf16[256,1024]{1,0:T(8,128)(2,1)S(1)} collective-permute-done((bf16[256,1024]{1,0:T(8,128)(2,1)S(1)}, bf16[256,1024]{1,0:T(8,128)(2,1)S(1)}, u32[]{:S(2)}, u32[]{:S(2)}) %collective-permute-start.81) | collective-permute-done | bytes 524320 | tf_op jit(solution)/shard_map/ppermute | solution.py:42
  515.8 8.3 %collective-permute-done.83 = bf16[64,1024]{1,0:T(8,128)(2,1)S(1)} collective-permute-done((bf16[64,1024]{1,0:T(8,128)(2,1)S(1)}, bf16[64,1024]{1,0:T(8,128)(2,1)S(1)}, u32[]{:S(2)}, u32[]{:S(2)}) %collective-permute-start.83) | collective-permute-done | bytes 131104 | tf_op jit(solution)/shard_map/ppermute | solution.py:42
  535.9 21.0 %expert_backward.6 = (bf16[512,1024]{1,0:T(8,128)(2,1)}, bf16[512,1024]{1,0:T(8,128)(2,1)}, bf16[1024,2048]{1,0:T(8,128)(2,1)}, bf16[1024,1024]{1,0:T(8,128)(2,1)}, bf16[1024,128]{1,0:T(8,128)(2,1)}) custom-call(f32[1024,128]{1,0:T(8,128)} %get-tuple-element.205.dep_ref, bf16[512,1024]{1,0:T(8,128)(2,1)} %copy-done.8, ...), custom_call_target="tpu_custom_call" | custom-call | flops 10737418240 | bytes 20000000 | tf_op jit(solution)/shard_map/expert_backward/pallas_call | solution.py:474
  556.9 21.0 %expert_backward.7 = (bf16[512,1024]{1,0:T(8,128)(2,1)}, bf16[512,1024]{1,0:T(8,128)(2,1)}, bf16[1024,2048]{1,0:T(8,128)(2,1)}, bf16[1024,1024]{1,0:T(8,128)(2,1)}, bf16[1024,128]{1,0:T(8,128)(2,1)}) custom-call(bf16[1024,128]{1,0:T(8,128)(2,1)} %get-tuple-element.210.dep_ref, bf16[512,1024]{1,0:T(8,128)(2,1)} %copy-done.6, ...), custom_call_target="tpu_custom_call" | custom-call | flops 10737418240 | bytes 20000000 | tf_op jit(solution)/shard_map/expert_backward/pallas_call | solution.py:474
  579.6 13.1 %expert_forward.7 = (bf16[512,1024]{1,0:T(8,128)(2,1)}, bf16[512,1024]{1,0:T(8,128)(2,1)}, f32[1024,128]{1,0:T(8,128)}) custom-call(bf16[1024,128]{1,0:T(8,128)(2,1)} %get-tuple-element.215.dep_ref, bf16[512,1024]{1,0:T(8,128)(2,1)} %copy-done.4, bf16[512,1024]{1,0:T(8,128)(2,1)} %collective-permute-done.58.xh_ref, ...), custom_call_target="tpu_custom_call" | custom-call | flops 6442450944 | bytes 12000000 | tf_op jit(solution)/shard_map/expert_forward/pallas_call | solution.py:451
  607.9 8.1 collective-permute-done.115
  630.5 7.8 collective-permute-done.107
  713.2 35.5 %conditional.1 = (f32[1,8,1024,128]{3,2,1,0:T(8,128)}, f32[1,8,1024,128]{3,2,1,0:T(8,128)}, f32[1,8,128,1024]{3,2,1,0:T(8,128)}) conditional(s32[]{:T(128)} %convert_element_type.989, (f32[8,1024,128]{2,1,0:T(8,128)}, f32[8,1024,128]{2,1,0:T(8,128)}, f32[8,128,1024]{2,1,0:T(8,128)}) %expert_weights.3, (bf16[512,1024]{1,0:T(8,128)(2,1)}, ...), branch_computations={%region_29.30_spmd, %region_30.31_spmd} | conditional | flops 12884901888 | bytes 56971572 | solution.py:712
  729.6 19.1 %expert_weights.2 = (f32[8,1024,128]{2,1,0:T(8,128)}, f32[8,1024,128]{2,1,0:T(8,128)}, f32[8,128,1024]{2,1,0:T(8,128)}) custom-call(f32[1,1024]{1,0:T(1,128)S(1)} %get-tuple-element.44.refs_0_, bf16[1024,512]{1,0:T(8,128)(2,1)} %bitcast.205, bf16[1024,512]{1,0:T(8,128)(2,1)} %bitcast.206, bf16[1024,512]{1,0:T(8,128)(2,1)} %bitcast.207, ...), custom_call_target="tpu_custom_call" | custom-call | flops 12884901888 | bytes 36000000 | tf_op jit(solution)/shard_map/cond/branch_1_fun/expert_weights/pallas_call | solution.py:498
  772.0 6.9 collective-permute-done.140
  788.5 6.9 collective-permute-done.148
  (803 shorter events, 523.1 us)
Async XLA Ops:
  7.2 800.9 %all-reduce.4.cloned.1.call-start = ((), (), s32[]{:S(2)}) async-start(), calls=%async_computation | async-start | bytes 262144 | tf_op jit(solution)/shard_map/psum | solution.py:725
  30.1 24.2 %collective-permute-start = (bf16[64,1024]{1,0:T(8,128)(2,1)}, bf16[64,1024]{1,0:T(8,128)(2,1)}, u32[]{:S(2)}, u32[]{:S(2)}) collective-permute-start(bf16[64,1024]{1,0:T(8,128)(2,1)} %get-tuple-element.165), channel_id=1, source_target_pairs={{0,1},{1,0},{2,3},{3,2},{4,5},{5,4},{6,7},{7,6},{8,9},{9,8},{10,11... | collective-permute-start | bytes 393224 | tf_op jit(solution)/shard_map/ppermute | solution.py:42
  62.6 25.6 %collective-permute-start.9 = (s32[512,8]{0,1:T(8,128)S(1)}, s32[512,8]{0,1:T(8,128)S(1)}, u32[]{:S(2)}, u32[]{:S(2)}) collective-permute-start(s32[512,8]{0,1:T(8,128)S(1)} %pad_add_fusion.2), channel_id=1, source_target_pairs={{0,4},{4,0},{8,12},{12,8},{1,5},{5,1},{9,13},{13,9},{2,6},{6,2},{1... | collective-permute-start | bytes 49160 | tf_op jit(solution)/shard_map/ppermute | solution.py:42
  135.8 47.6 %collective-permute-start.46 = (bf16[64,1024]{1,0:T(8,128)(2,1)S(1)}, bf16[64,1024]{1,0:T(8,128)(2,1)S(1)}, u32[]{:S(2)}, u32[]{:S(2)}) collective-permute-start(bf16[64,1024]{1,0:T(8,128)(2,1)S(1)} %get-tuple-element.420), channel_id=1, source_target_pairs={{0,1},{1,0},{2,3},{3,2},{4,5},{5,4},{6,7},{7,6},{8,9},{9,8},{10,11... | collective-permute-start | bytes 393224 | tf_op jit(solution)/shard_map/ppermute | solution.py:42
  142.7 75.6 %collective-permute-start.47 = (bf16[64,1024]{1,0:T(8,128)(2,1)S(1)}, bf16[64,1024]{1,0:T(8,128)(2,1)S(1)}, u32[]{:S(2)}, u32[]{:S(2)}) collective-permute-start(bf16[64,1024]{1,0:T(8,128)(2,1)S(1)} %get-tuple-element.420), channel_id=1, source_target_pairs={{0,2},{1,3},{2,0},{3,1},{4,6},{5,7},{6,4},{7,5},{8,10},{9,11},{10,... | collective-permute-start | bytes 393224 | tf_op jit(solution)/shard_map/ppermute | solution.py:42
  187.2 24.0 %collective-permute-start.39 = (bf16[64,1024]{1,0:T(8,128)(2,1)S(1)}, bf16[64,1024]{1,0:T(8,128)(2,1)S(1)}, u32[]{:S(2)}, u32[]{:S(2)}) collective-permute-start(bf16[64,1024]{1,0:T(8,128)(2,1)S(1)} %collective-permute-done.37.refs_1_.refs_5_), channel_id=1, source_target_pairs={{0,2},{1,3},{2,0},{3,1},{4,6},{5,7},{6,4},{7,5},{8,10},{9,11},{10,... | collective-permute-start | bytes 393224 | tf_op jit(solution)/shard_map/ppermute | solution.py:42
  197.1 23.6 %collective-permute-start.48 = (bf16[64,1024]{1,0:T(8,128)(2,1)S(1)}, bf16[64,1024]{1,0:T(8,128)(2,1)S(1)}, u32[]{:S(2)}, u32[]{:S(2)}) collective-permute-start(bf16[64,1024]{1,0:T(8,128)(2,1)S(1)} %get-tuple-element.420), channel_id=1, source_target_pairs={{0,3},{1,2},{2,1},{3,0},{4,7},{5,6},{6,5},{7,4},{8,11},{9,10},{10,... | collective-permute-start | bytes 393224 | tf_op jit(solution)/shard_map/ppermute | solution.py:42
  229.5 31.4 %collective-permute-start.49 = (bf16[256,1024]{1,0:T(8,128)(2,1)S(1)}, bf16[256,1024]{1,0:T(8,128)(2,1)S(1)}, u32[]{:S(2)}, u32[]{:S(2)}) collective-permute-start(bf16[256,1024]{1,0:T(8,128)(2,1)S(1)} %pad_maximum_fusion.4), channel_id=1, source_target_pairs={{0,8},{4,12},{8,0},{12,4},{1,9},{5,13},{9,1},{13,5},{2,10},{6,14},... | collective-permute-start | bytes 1572872 | tf_op jit(solution)/shard_map/ppermute | solution.py:42
  231.0 46.6 %collective-permute-start.62 = (bf16[256,1024]{1,0:T(8,128)(2,1)S(1)}, bf16[256,1024]{1,0:T(8,128)(2,1)S(1)}, u32[]{:S(2)}, u32[]{:S(2)}) collective-permute-start(bf16[256,1024]{1,0:T(8,128)(2,1)S(1)} %pad_maximum_fusion.6), channel_id=1, source_target_pairs={{0,8},{4,12},{8,0},{12,4},{1,9},{5,13},{9,1},{13,5},{2,10},{6,14},... | collective-permute-start | bytes 1572872 | tf_op jit(solution)/shard_map/ppermute | solution.py:42
  260.9 25.6 %collective-permute-start.50 = (bf16[512,1024]{1,0:T(8,128)(2,1)S(1)}, bf16[512,1024]{1,0:T(8,128)(2,1)S(1)}, u32[]{:S(2)}, u32[]{:S(2)}) collective-permute-start(bf16[512,1024]{1,0:T(8,128)(2,1)S(1)} %constant_dynamic-update-slice_fusion.15.gl_ref.refs_5_), channel_id=1, source_target_pairs={{0,4},{4,0},{8,12},{12,8},{1,5},{5,1},{9,13},{13,9},{2,6},{6,2},{1... | collective-permute-start | bytes 3145736 | tf_op jit(solution)/shard_map/ppermute | solution.py:42
  278.5 31.3 %collective-permute-start.63 = (bf16[512,1024]{1,0:T(8,128)(2,1)}, bf16[512,1024]{1,0:T(8,128)(2,1)}, u32[]{:S(2)}, u32[]{:S(2)}) collective-permute-start(bf16[512,1024]{1,0:T(8,128)(2,1)} %constant_dynamic-update-slice_fusion.25.gl_ref.refs_7_), channel_id=1, source_target_pairs={{0,4},{4,0},{8,12},{12,8},{1,5},{5,1},{9,13},{13,9},{2,6},{6,2},{1... | collective-permute-start | bytes 3145736 | tf_op jit(solution)/shard_map/ppermute | solution.py:42
  436.6 24.4 %collective-permute-start.90 = (bf16[64,1024]{1,0:T(8,128)(2,1)}, bf16[64,1024]{1,0:T(8,128)(2,1)S(1)}, u32[]{:S(2)}, u32[]{:S(2)}) collective-permute-start(bf16[64,1024]{1,0:T(8,128)(2,1)} %get-tuple-element.209), channel_id=1, source_target_pairs={{0,3},{1,2},{2,1},{3,0},{4,7},{5,6},{6,5},{7,4},{8,11},{9,10},{10,... | collective-permute-start | bytes 393224 | tf_op jit(solution)/shard_map/ppermute | solution.py:42
  460.8 28.1 %collective-permute-start.80 = (bf16[512,1024]{1,0:T(8,128)(2,1)S(1)}, bf16[512,1024]{1,0:T(8,128)(2,1)S(1)}, u32[]{:S(2)}, u32[]{:S(2)}) collective-permute-start(bf16[512,1024]{1,0:T(8,128)(2,1)S(1)} %copy-done.131), channel_id=1, source_target_pairs={{0,4},{4,0},{8,12},{12,8},{1,5},{5,1},{9,13},{13,9},{2,6},{6,2},{1... | collective-permute-start | bytes 3145736 | tf_op jit(solution)/shard_map/ppermute | solution.py:42
  487.2 26.7 %collective-permute-start.95 = (bf16[256,1024]{1,0:T(8,128)(2,1)S(1)}, bf16[256,1024]{1,0:T(8,128)(2,1)S(1)}, u32[]{:S(2)}, u32[]{:S(2)}) collective-permute-start(bf16[256,1024]{1,0:T(8,128)(2,1)S(1)} %pad_maximum_fusion.8), channel_id=1, source_target_pairs={{0,8},{4,12},{8,0},{12,4},{1,9},{5,13},{9,1},{13,5},{2,10},{6,14},... | collective-permute-start | bytes 1572872 | tf_op jit(solution)/shard_map/ppermute | solution.py:42
  492.7 36.6 %collective-permute-start.104 = (bf16[256,1024]{1,0:T(8,128)(2,1)S(1)}, bf16[256,1024]{1,0:T(8,128)(2,1)S(1)}, u32[]{:S(2)}, u32[]{:S(2)}) collective-permute-start(bf16[256,1024]{1,0:T(8,128)(2,1)S(1)} %pad_maximum_fusion.9), channel_id=1, source_target_pairs={{0,8},{4,12},{8,0},{12,4},{1,9},{5,13},{9,1},{13,5},{2,10},{6,14},... | collective-permute-start | bytes 1572872 | tf_op jit(solution)/shard_map/ppermute | solution.py:42
  530.1 26.8 %collective-permute-start.105 = (bf16[512,1024]{1,0:T(8,128)(2,1)}, bf16[512,1024]{1,0:T(8,128)(2,1)}, u32[]{:S(2)}, u32[]{:S(2)}) collective-permute-start(bf16[512,1024]{1,0:T(8,128)(2,1)} %constant_dynamic-update-slice_fusion.35.gl_ref), channel_id=1, source_target_pairs={{0,4},{4,0},{8,12},{12,8},{1,5},{5,1},{9,13},{13,9},{2,6},{6,2},{1... | collective-permute-start | bytes 3145736 | tf_op jit(solution)/shard_map/ppermute | solution.py:42
  605.5 32.9 %collective-permute-start.107 = (bf16[256,1024]{1,0:T(8,128)(2,1)}, bf16[256,1024]{1,0:T(8,128)(2,1)}, u32[]{:S(2)}, u32[]{:S(2)}) collective-permute-start(bf16[256,1024]{1,0:T(8,128)(2,1)} %get-tuple-element.365), channel_id=1, source_target_pairs={{0,8},{4,12},{8,0},{12,4},{1,9},{5,13},{9,1},{13,5},{2,10},{6,14},... | collective-permute-start | bytes 1572872 | tf_op jit(solution)/shard_map/ppermute | solution.py:42
  618.9 25.1 %collective-permute-start.116 = (bf16[64,1024]{1,0:T(8,128)(2,1)S(1)}, bf16[64,1024]{1,0:T(8,128)(2,1)S(1)}, u32[]{:S(2)}, u32[]{:S(2)}) collective-permute-start(bf16[64,1024]{1,0:T(8,128)(2,1)S(1)} %get-tuple-element.378), channel_id=1, source_target_pairs={{0,1},{1,0},{2,3},{3,2},{4,5},{5,4},{6,7},{7,6},{8,9},{9,8},{10,11... | collective-permute-start | bytes 393224 | tf_op jit(solution)/shard_map/ppermute | solution.py:42
  669.1 26.2 %collective-permute-start.113 = (bf16[64,1024]{1,0:T(8,128)(2,1)S(1)}, bf16[64,1024]{1,0:T(8,128)(2,1)S(1)}, u32[]{:S(2)}, u32[]{:S(2)}) collective-permute-start(bf16[64,1024]{1,0:T(8,128)(2,1)S(1)} %fusion.29), channel_id=1, source_target_pairs={{0,3},{1,2},{2,1},{3,0},{4,7},{5,6},{6,5},{7,4},{8,11},{9,10},{10,... | collective-permute-start | bytes 393224 | tf_op jit(solution)/shard_map/ppermute | solution.py:42
  697.1 52.6 %collective-permute-start.138 = (bf16[64,1024]{1,0:T(8,128)(2,1)}, bf16[64,1024]{1,0:T(8,128)(2,1)}, u32[]{:S(2)}, u32[]{:S(2)}) collective-permute-start(bf16[64,1024]{1,0:T(8,128)(2,1)} %get-tuple-element.231), channel_id=1, source_target_pairs={{0,3},{1,2},{2,1},{3,0},{4,7},{5,6},{6,5},{7,4},{8,11},{9,10},{10,... | collective-permute-start | bytes 393224 | tf_op jit(solution)/shard_map/ppermute | solution.py:42
  699.3 53.2 %collective-permute-start.137 = (bf16[64,1024]{1,0:T(8,128)(2,1)}, bf16[64,1024]{1,0:T(8,128)(2,1)}, u32[]{:S(2)}, u32[]{:S(2)}) collective-permute-start(bf16[64,1024]{1,0:T(8,128)(2,1)} %get-tuple-element.230), channel_id=1, source_target_pairs={{0,2},{1,3},{2,0},{3,1},{4,6},{5,7},{6,4},{7,5},{8,10},{9,11},{10,... | collective-permute-start | bytes 393224 | tf_op jit(solution)/shard_map/ppermute | solution.py:42
  704.5 48.0 %collective-permute-start.136 = (bf16[64,1024]{1,0:T(8,128)(2,1)}, bf16[64,1024]{1,0:T(8,128)(2,1)}, u32[]{:S(2)}, u32[]{:S(2)}) collective-permute-start(bf16[64,1024]{1,0:T(8,128)(2,1)} %get-tuple-element.229), channel_id=1, source_target_pairs={{0,1},{1,0},{2,3},{3,2},{4,5},{5,4},{6,7},{7,6},{8,9},{9,8},{10,11... | collective-permute-start | bytes 393224 | tf_op jit(solution)/shard_map/ppermute | solution.py:42
  706.3 46.2 %collective-permute-start.124 = (bf16[64,1024]{1,0:T(8,128)(2,1)}, bf16[64,1024]{1,0:T(8,128)(2,1)}, u32[]{:S(2)}, u32[]{:S(2)}) collective-permute-start(bf16[64,1024]{1,0:T(8,128)(2,1)} %get-tuple-element.224), channel_id=1, source_target_pairs={{0,3},{1,2},{2,1},{3,0},{4,7},{5,6},{6,5},{7,4},{8,11},{9,10},{10,... | collective-permute-start | bytes 393224 | tf_op jit(solution)/shard_map/ppermute | solution.py:42
  712.1 36.7 %collective-permute-start.146 = (f32[2,1024]{1,0:T(2,128)S(1)}, f32[2,1024]{1,0:T(2,128)}, u32[]{:S(2)}, u32[]{:S(2)}) collective-permute-start(f32[2,1024]{1,0:T(2,128)S(1)} %add.738), channel_id=1, source_target_pairs={{0,4},{4,0},{8,12},{12,8},{1,5},{5,1},{9,13},{13,9},{2,6},{6,2},{1... | collective-permute-start | bytes 24584 | tf_op jit(solution)/shard_map/ppermute | solution.py:42
  (268 other events, 3869.2 us)
Sparse Core Ops, SparseCore 0:
  608.0 98.1 all-reduce.3

commit v2 on v1

v2 whole, which is shorter than its diff:
```python
import functools

import jax
import jax.numpy as jnp
from jax import lax
from jax.experimental import pallas as pl
from jax.experimental.pallas import tpu as pltpu
from jax.sharding import PartitionSpec as P

QUERY_HEADS = 16
KEY_VALUE_HEADS = 8
HEAD_SIZE = 64
NE = 32
SLOTS = 4
LANES = 128

EPSILON = 1e-06
THETA_BASE = 10000.0
MASKED = -1e30
TILE = 256
GROUPS = QUERY_HEADS // KEY_VALUE_HEADS
SCORE_SCALE = HEAD_SIZE ** (-0.5)
VMEM_LIMIT = 60 * 1024 * 1024

f32 = jnp.float32
bf16 = jnp.bfloat16


def dot_nn(a, b):
    return lax.dot_general(a, b, (((1,), (0,)), ((), ())), preferred_element_type=f32)


def dot_nt(a, b):
    return lax.dot_general(a, b, (((1,), (1,)), ((), ())), preferred_element_type=f32)


def dot_tn(a, b):
    return lax.dot_general(a, b, (((0,), (0,)), ((), ())), preferred_element_type=f32)


def swap(x, axis, k):
    return lax.ppermute(x, axis, [(i, i ^ k) for i in range(lax.axis_size(axis))])


def shifted(x, by):
    length = lax.axis_size("section")
    return lax.ppermute(x, "section", [(i, i + by) for i in range(length) if 0 <= i + by < length])


def expert_bits():
    n = lax.axis_size("expert")
    bits = []
    k = n // 2
    while k >= 1:
        bits.append(k)
        k //= 2
    return bits


def pieces_tensor(x):
    return [x] + [swap(x, "tensor", k) for k in range(1, lax.axis_size("tensor"))]


def after(value, *others):
    return lax.optimization_barrier((value, *others))[0]


def gather_far(own):
    blocks = [own]
    for k in expert_bits()[:-1]:
        blocks = blocks + [swap(block, "expert", k) for block in blocks]
    return blocks


def pair(block):
    return (block, swap(block, "expert", 1))


def gather_pairs(own):
    return [pair(block) for block in gather_far(own)]


def added(terms):
    return sum(term.astype(f32) for term in terms).astype(bf16)


def reduce_pairs(pairs):
    bits = expert_bits()
    terms = [[block, swap(other, "expert", bits[-1])] for block, other in pairs]
    sent = terms[0][0]
    for k in reversed(bits[:-1]):
        half = len(terms) // 2
        for j in range(half):
            sent = added(terms[half + j])
            terms[j].append(swap(sent, "expert", k))
        terms = terms[:half]
    return terms[0], sent


def reduce_pieces(pieces, *done):
    got = [swap(pieces[k], "tensor", k) for k in range(1, len(pieces))]
    if done:
        got[-1] = after(got[-1], *done)
    return sum((g.astype(f32) for g in got), pieces[0].astype(f32))


def gather_weight(w):
    low = (lax.axis_index("expert") & 1) == 0
    half = w.shape[0] // 2
    mine = jnp.where(low, w[:half], w[half:])
    far = jnp.concatenate(pieces_tensor(mine)[1:], axis=0)
    near = swap(far, "expert", 1)
    out = [w]
    for k in range(lax.axis_size("tensor") - 1):
        cut = slice(k * half, (k + 1) * half)
        out.append(jnp.where(low, far[cut], near[cut]))
        out.append(jnp.where(low, near[cut], far[cut]))
    return jnp.concatenate(out, axis=0)


def sum_expert(y):
    bits = list(reversed(expert_bits()))
    for k in bits:
        half = y.shape[0] // 2
        low = (lax.axis_index("expert") & k) == 0
        mine = jnp.where(low, y[:half], y[half:])
        other = jnp.where(low, y[half:], y[:half])
        y = (mine.astype(f32) + swap(other, "expert", k).astype(f32)).astype(y.dtype)
    for k in reversed(bits):
        low = (lax.axis_index("expert") & k) == 0
        theirs = swap(y, "expert", k)
        y = jnp.concatenate([jnp.where(low, y, theirs), jnp.where(low, theirs, y)], axis=0)
    return y


def sum_all_small(y):
    n = lax.axis_size("tensor")
    y = y + sum(swap(y, "tensor", k) for k in range(1, n))
    for k in expert_bits():
        y = y + swap(y, "expert", k)
    return y


def relative(x, axis, index, count):
    shape = x.shape
    k = count // 2
    while k >= 1:
        outer = count // (2 * k)
        inner = shape[axis] // (outer * 2)
        view = x.reshape(shape[:axis] + (outer, 2, inner) + shape[axis + 1 :])
        flipped = jnp.flip(view, axis=axis + 1)
        x = jnp.where((index & k) != 0, flipped, view).reshape(shape)
        k //= 2
    return x


def rope(v, cosine, sine):
    lane = lax.broadcasted_iota(jnp.int32, v.shape, 1) % HEAD_SIZE
    width = v.shape[1]
    left = pltpu.roll(v, width - HEAD_SIZE // 2, 1)
    right = pltpu.roll(v, HEAD_SIZE // 2, 1)
    return v * cosine + jnp.where(lane < HEAD_SIZE // 2, left, right) * sine


def rope_t(g, cosine, sine):
    return rope(g, cosine, -sine)


def twice(v, upper):
    lane = lax.broadcasted_iota(jnp.int32, v.shape, 1)
    keep = lane >= HEAD_SIZE if upper else lane < HEAD_SIZE
    return jnp.where(keep, v, pltpu.roll(v, HEAD_SIZE, 1))


def halves(v):
    lane = lax.broadcasted_iota(jnp.int32, v.shape, 1)
    return (jnp.where(lane < HEAD_SIZE, v, 0.0), jnp.where(lane >= HEAD_SIZE, v, 0.0))


def both(low, high):
    lane = lax.broadcasted_iota(jnp.int32, low.shape, 1)
    return jnp.where(lane < HEAD_SIZE, low, high)


def attn_forward_kernel(count, *refs):
    x_refs = refs[1 : 1 + count]
    gain_ref, wqkv_ref, cos_ref, sin_ref, mask_ref = refs[1 + count : 6 + count]
    mixed_ref, qkv_ref, normed_ref = refs[6 + count :]
    x = jnp.concatenate([r[...] for r in x_refs], axis=0).astype(f32)
    scale = lax.rsqrt(jnp.mean(x * x, axis=-1, keepdims=True) + EPSILON)
    normed = (x * scale * gain_ref[...]).astype(bf16)
    normed_ref[...] = normed
    qkv = dot_nn(normed, wqkv_ref[...])
    cosine, sine = cos_ref[0], sin_ref[0]
    q_width = mixed_ref.shape[1]
    kv_width = (qkv.shape[1] - q_width) // 2
    groups = []
    for at in range(0, qkv.shape[1], 128):
        piece = qkv[:, at : at + 128]
        if at < q_width + kv_width:
            piece = rope(piece, cosine, sine)
        piece = piece.astype(bf16)
        qkv_ref[:, at : at + 128] = piece
        groups.append(piece.astype(f32))
    allowed = mask_ref[0] > 0.0
    mixed = []
    for g in range(kv_width // HEAD_SIZE):
        k = twice(groups[q_width // 128 + g // 2], g % 2).astype(bf16)
        v = twice(groups[(q_width + kv_width) // 128 + g // 2], g % 2).astype(bf16)
        outs = []
        for q in halves(groups[g]):
            s = jnp.where(allowed, dot_nt(q.astype(bf16), k) * SCORE_SCALE, MASKED)
            p = jnp.exp(s - jnp.max(s, axis=-1, keepdims=True))
            p = (p / jnp.sum(p, axis=-1, keepdims=True)).astype(bf16)
            outs.append(dot_nn(p, v))
        mixed.append(both(*outs).astype(bf16))
    mixed_ref[...] = jnp.concatenate(mixed, axis=1)


def attn_project_kernel(count, *refs):
    mixed_refs = refs[1 : 1 + count]
    x_refs = refs[1 + count : 1 + 2 * count]
    wo_ref, gain_ref, rows_ref, middle_ref = refs[1 + 2 * count :]
    part = x_refs[0].shape[0]
    mixed = jnp.concatenate(
        [
            jnp.concatenate([r[(i ^ k) * part : ((i ^ k) + 1) * part, :] for i in range(count)], axis=0)
            for k, r in enumerate(mixed_refs)
        ],
        axis=1,
    )
    x = jnp.concatenate([r[...] for r in x_refs], axis=0).astype(f32)
    middle = x + dot_nn(mixed, wo_ref[...])
    scale = lax.rsqrt(jnp.mean(middle * middle, axis=-1, keepdims=True) + EPSILON)
    rows_ref[...] = (middle * scale * gain_ref[...]).astype(bf16)
    middle_ref[...] = middle[: middle_ref.shape[0]]


def split_kernel(terms, *refs):
    total = sum(r[...].astype(f32) for r in refs[1 : 1 + terms]).astype(bf16)
    outs = refs[1 + terms :]
    rows = total.shape[0] // len(outs)
    for j, out in enumerate(outs):
        out[...] = total[j * rows : (j + 1) * rows]


def attn_backward_kernel(count, *refs):
    gm_refs = refs[1 : 1 + count]
    x_refs = refs[1 + count : 1 + 2 * count]
    qkv_ref, wqkv_ref, wo_ref, cos_ref, sin_ref, mask_ref = refs[1 + 2 * count : 7 + 2 * count]
    part_refs = refs[7 + 2 * count : 7 + 3 * count]
    gqkv_ref, gain_ref, gm_ref = refs[7 + 3 * count :]
    gm = jnp.concatenate([r[...] for r in gm_refs], axis=0)
    gm_ref[...] = gm
    cosine, sine = cos_ref[0], sin_ref[0]
    q_width = wo_ref.shape[0]
    kv_width = (qkv_ref.shape[1] - q_width) // 2
    gmix = dot_nt(gm, wo_ref[...]).astype(bf16).astype(f32)
    allowed = mask_ref[0] > 0.0
    grads = [None] * (qkv_ref.shape[1] // 128)
    for g in range(kv_width // HEAD_SIZE):
        k_at = q_width // 128 + g // 2
        v_at = (q_width + kv_width) // 128 + g // 2
        k = twice(qkv_ref[:, k_at * 128 : k_at * 128 + 128].astype(f32), g % 2).astype(bf16)
        v = twice(qkv_ref[:, v_at * 128 : v_at * 128 + 128].astype(f32), g % 2).astype(bf16)
        qs = halves(qkv_ref[:, g * 128 : g * 128 + 128].astype(f32))
        gxs = halves(gmix[:, g * 128 : g * 128 + 128])
        gqs, gk, gv = [], None, None
        for q, gx in zip(qs, gxs):
            q, gx = q.astype(bf16), gx.astype(bf16)
            s = jnp.where(allowed, dot_nt(q, k) * SCORE_SCALE, MASKED)
            p = jnp.exp(s - jnp.max(s, axis=-1, keepdims=True))
            p = p / jnp.sum(p, axis=-1, keepdims=True)
            gp = dot_nt(gx, v)
            gs = p * (gp - jnp.sum(p * gp, axis=-1, keepdims=True))
            gqs.append(dot_nn(gs.astype(bf16), k) * SCORE_SCALE)
            gk_h = dot_nn(gs.T.astype(bf16), q)
            gv_h = dot_nn(p.T.astype(bf16), gx)
            gk = gk_h if gk is None else gk + gk_h
            gv = gv_h if gv is None else gv + gv_h
        grads[g] = both(*gqs)
        gk = (gk + pltpu.roll(gk, HEAD_SIZE, 1)) * SCORE_SCALE
        gv = gv + pltpu.roll(gv, HEAD_SIZE, 1)
        grads[k_at] = gk if g % 2 == 0 else both(grads[k_at], gk)
        grads[v_at] = gv if g % 2 == 0 else both(grads[v_at], gv)
    for j in range(len(grads)):
        piece = grads[j]
        if j * 128 < q_width + kv_width:
            piece = rope_t(piece, cosine, sine)
        grads[j] = piece.astype(bf16)
    gqkv = jnp.concatenate(grads, axis=1)
    gqkv_ref[...] = gqkv
    part = dot_nt(gqkv, wqkv_ref[...])
    rows = part.shape[0] // count
    for j in range(count):
        part_refs[j][...] = part[j * rows : (j + 1) * rows].astype(bf16)
    x = jnp.concatenate([r[...] for r in x_refs], axis=0).astype(f32)
    scale = lax.rsqrt(jnp.mean(x * x, axis=-1, keepdims=True) + EPSILON)
    gain_ref[0] = jnp.sum(part * x * scale, axis=0, keepdims=True)


def pick(first_ref, second_ref, steps):
    return jnp.where(pl.program_id(0) < steps // 2, first_ref[...], second_ref[...])


def put(first_ref, second_ref, steps, value):
    @pl.when(pl.program_id(0) < steps // 2)
    def _():
        first_ref[...] = value

    @pl.when(pl.program_id(0) >= steps // 2)
    def _():
        second_ref[...] = value


def expert_forward_kernel(
    steps, dep_ref, xa_ref, xb_ref, sa_ref, sb_ref, wr_ref, wg_ref, wu_ref, wd_ref,
    oa_ref, ob_ref,
):
    x = pick(xa_ref, xb_ref, steps)
    sel = pick(sa_ref, sb_ref, steps)
    width = wd_ref.shape[0]
    count = width // 128
    logits = jnp.where(sel > 0.0, dot_nn(x, wr_ref[...]), MASKED)
    probs = jnp.exp(logits - jnp.max(logits, axis=-1, keepdims=True)) * sel
    probs = probs / jnp.maximum(jnp.sum(probs, axis=-1, keepdims=True), 1e-30)
    hidden = []
    for e in range(count):
        h = dot_nn(x, jnp.concatenate([wg_ref[e], wu_ref[e]], axis=1))
        gate, up = h[:, :128], h[:, 128:]
        hidden.append((gate * jax.nn.sigmoid(gate) * up * probs[:, e : e + 1]).astype(bf16))
    out = dot_nn(jnp.concatenate(hidden, axis=1), wd_ref[...]).astype(bf16)
    put(oa_ref, ob_ref, steps, out)


def expert_backward_kernel(
    steps, dep_ref, xa_ref, xb_ref, ga_ref, gb_ref, sa_ref, sb_ref, wr_ref, wg_ref, wu_ref, wd_ref,
    oa_ref, ob_ref, act_ref, hid_ref, xt_ref, glog_ref,
):
    x = pick(xa_ref, xb_ref, steps)
    gy = pick(ga_ref, gb_ref, steps)
    sel = pick(sa_ref, sb_ref, steps)
    xt_ref[...] = x.astype(f32).T.astype(bf16)
    width = wd_ref.shape[0]
    count = width // 128
    logits = jnp.where(sel > 0.0, dot_nn(x, wr_ref[...]), MASKED)
    probs = jnp.exp(logits - jnp.max(logits, axis=-1, keepdims=True)) * sel
    probs = probs / jnp.maximum(jnp.sum(probs, axis=-1, keepdims=True), 1e-30)
    lane = lax.broadcasted_iota(jnp.int32, probs.shape, 1)
    grad_act = dot_nt(gy, wd_ref[...])
    grad_gates = jnp.zeros(probs.shape, f32)
    pieces = []
    for e in range(count):
        h = dot_nn(x, jnp.concatenate([wg_ref[e], wu_ref[e]], axis=1))
        gate, up = h[:, :128], h[:, 128:]
        s = jax.nn.sigmoid(gate)
        silu = gate * s
        hid = silu * up
        ga = grad_act[:, e * 128 : (e + 1) * 128]
        p = probs[:, e : e + 1]
        grad_gates = jnp.where(
            lane == e, jnp.sum(hid * ga, axis=-1, keepdims=True), grad_gates
        )
        gp = ga * p
        pieces.append((gp * up * s * (1.0 + gate * (1.0 - s))).astype(bf16))
        pieces.append((gp * silu).astype(bf16))
        hid_ref[e * 128 : (e + 1) * 128, :] = (hid * p).T.astype(bf16)
    gcat = jnp.concatenate(pieces, axis=1)
    act_ref[...] = gcat
    glog = probs * (grad_gates - jnp.sum(probs * grad_gates, axis=-1, keepdims=True))
    glog = glog.astype(bf16)
    glog_ref[...] = glog
    wcat = jnp.concatenate([w[e] for e in range(count) for w in (wg_ref, wu_ref)], axis=1)
    out = (dot_nt(gcat, wcat) + dot_nt(glog, wr_ref[...])).astype(bf16)
    put(oa_ref, ob_ref, steps, out)


def expert_weights_kernel(pairs, *refs):
    xt_refs = refs[1 : 1 + pairs]
    gy_refs = refs[1 + pairs : 1 + 3 * pairs]
    act_refs = refs[1 + 3 * pairs : 1 + 4 * pairs]
    hid_refs = refs[1 + 4 * pairs : 1 + 5 * pairs]
    glog_refs = refs[1 + 5 * pairs : 1 + 6 * pairs]
    gate_ref, up_ref, down_ref, router_ref = refs[1 + 6 * pairs :]
    rows = gy_refs[0].shape[0]

    @pl.when(pl.program_id(0) == 0)
    def _():
        for at in range(0, xt_refs[0].shape[0], 256):
            router_ref[at : at + 256, :] = sum(
                dot_nn(xt_refs[j][at : at + 256, :], glog_refs[j][...]) for j in range(pairs)
            )

    for at in range(0, xt_refs[0].shape[0], 256):
        grads = sum(dot_nn(xt_refs[j][at : at + 256, :], act_refs[j][...]) for j in range(pairs))
        for j in range(grads.shape[1] // 256):
            gate_ref[j, at : at + 256, :] = grads[:, j * 256 : j * 256 + 128]
            up_ref[j, at : at + 256, :] = grads[:, j * 256 + 128 : j * 256 + 256]
    down = sum(
        dot_nn(hid_refs[j // 2][:, (j % 2) * rows : (j % 2 + 1) * rows], gy_refs[j][...])
        for j in range(2 * pairs)
    )
    for j in range(down.shape[0] // 128):
        down_ref[j] = down[j * 128 : (j + 1) * 128, :]


def full(array):
    zeros = (0,) * array.ndim
    return pl.BlockSpec(array.shape, lambda *_: zeros)


def once(array):
    zeros = (0,) * array.ndim
    return pl.BlockSpec(array.shape, lambda *_: zeros, pipeline_mode=pl.Buffered(1))


ANYWHERE = pl.BlockSpec(memory_space=pl.ANY)


def params():
    return pltpu.CompilerParams(vmem_limit_bytes=VMEM_LIMIT)


def cost(flops, moved):
    return pl.CostEstimate(flops=int(flops), bytes_accessed=int(moved), transcendentals=0)


def by_micro(array, micro_count):
    if array.ndim == 3:
        return pl.BlockSpec((1,) + array.shape[1:], lambda m: (m, 0, 0))
    return pl.BlockSpec((array.shape[0] // micro_count, array.shape[1]), lambda m: (m, 0))


def attn_forward(dep, xs, gain, wqkv, q_width, cosine, sine, mask):
    count = len(xs)
    micro_count = mask.shape[0]
    width = xs[0].shape[1]
    rows = xs[0].shape[0] * count
    heads = wqkv.shape[1]
    split = lambda array: by_micro(array, micro_count)
    outs = (
        jax.ShapeDtypeStruct((rows, q_width), bf16),
        jax.ShapeDtypeStruct((rows, heads), bf16),
        jax.ShapeDtypeStruct((rows, width), bf16),
    )
    return pl.pallas_call(
        functools.partial(attn_forward_kernel, count),
        out_shape=outs,
        grid=(micro_count,),
        in_specs=[ANYWHERE]
        + [split(x) for x in xs]
        + [full(gain), full(wqkv), split(cosine), split(sine), split(mask)],
        out_specs=[split(o) for o in outs],
        compiler_params=params(),
        cost_estimate=cost(2 * rows * width * heads, 6e6),
        name="attn_forward",
    )(dep, *xs, gain, wqkv, cosine, sine, mask)


def attn_project(dep, mixed, xs, wo, gain, micro_count):
    count = len(xs)
    width = xs[0].shape[1]
    rows = xs[0].shape[0] * count
    split = lambda array: by_micro(array, micro_count)
    outs = (
        jax.ShapeDtypeStruct((rows, width), bf16),
        jax.ShapeDtypeStruct((rows // count, width), f32),
    )
    return pl.pallas_call(
        functools.partial(attn_project_kernel, count),
        out_shape=outs,
        grid=(micro_count,),
        in_specs=[ANYWHERE]
        + [split(x) for x in mixed]
        + [split(x) for x in xs]
        + [full(wo), full(gain)],
        out_specs=[split(o) for o in outs],
        compiler_params=params(),
        cost_estimate=cost(2 * rows * width * width, 6e6),
        name="attn_project",
    )(dep, *mixed, *xs, wo, gain)


def split_sum(dep, terms, count, micro_count):
    rows, width = terms[0].shape
    split = lambda array: by_micro(array, micro_count)
    outs = (jax.ShapeDtypeStruct((rows // count, width), bf16),) * count
    return pl.pallas_call(
        functools.partial(split_kernel, len(terms)),
        out_shape=outs,
        grid=(micro_count,),
        in_specs=[ANYWHERE] + [split(x) for x in terms],
        out_specs=[split(o) for o in outs],
        compiler_params=params(),
        cost_estimate=cost(rows * width * 4, 4e6),
        name="split_sum",
    )(dep, *terms)


def attn_backward(dep, gms, xs, qkv, wqkv, wo, cosine, sine, mask):
    count = len(xs)
    micro_count = mask.shape[0]
    part, width = xs[0].shape
    rows = part * count
    heads = wqkv.shape[1]
    split = lambda array: by_micro(array, micro_count)
    outs = (jax.ShapeDtypeStruct((part, width), bf16),) * count + (
        jax.ShapeDtypeStruct((rows, heads), bf16),
        jax.ShapeDtypeStruct((micro_count, 1, width), f32),
        jax.ShapeDtypeStruct((rows, width), bf16),
    )
    out = pl.pallas_call(
        functools.partial(attn_backward_kernel, count),
        out_shape=outs,
        grid=(micro_count,),
        in_specs=[ANYWHERE]
        + [split(x) for x in gms]
        + [split(x) for x in xs]
        + [split(qkv), full(wqkv), full(wo), split(cosine), split(sine), split(mask)],
        out_specs=[split(o) for o in outs],
        compiler_params=params(),
        cost_estimate=cost(2 * rows * width * (heads + wo.shape[0]), 8e6),
        name="attn_backward",
    )(dep, *gms, *xs, qkv, wqkv, wo, cosine, sine, mask)
    return (out[:count], *out[count:])


def pair_specs(rows):
    half = rows // TILE
    first = lambda w: pl.BlockSpec((TILE, w), lambda i: (jnp.minimum(i, half - 1), 0))
    second = lambda w: pl.BlockSpec((TILE, w), lambda i: (jnp.maximum(i - half, 0), 0))
    whole = lambda w: pl.BlockSpec((TILE, w), lambda i: (i, 0))
    return (first, second, whole)


def expert_forward(dep, x, sel, wr, wg, wu, wd):
    rows, width = x[0].shape
    steps = 2 * rows // TILE
    first, second, whole = pair_specs(rows)
    outs = (jax.ShapeDtypeStruct((rows, width), bf16),) * 2
    return pl.pallas_call(
        functools.partial(expert_forward_kernel, steps),
        out_shape=outs,
        grid=(steps,),
        in_specs=[ANYWHERE, first(width), second(width), first(LANES), second(LANES)]
        + [once(wr), once(wg), once(wu), once(wd)],
        out_specs=[first(width), second(width)],
        compiler_params=params(),
        cost_estimate=cost(4 * rows * 3 * wg.size, 12e6),
        name="expert_forward",
    )(dep, *x, *sel, wr, wg, wu, wd)


def expert_backward(dep, x, gy, sel, wr, wg, wu, wd):
    rows, width = x[0].shape
    steps = 2 * rows // TILE
    first, second, whole = pair_specs(rows)
    across = lambda h: pl.BlockSpec((h, TILE), lambda i: (0, i))
    outs = (
        jax.ShapeDtypeStruct((rows, width), bf16),
        jax.ShapeDtypeStruct((rows, width), bf16),
        jax.ShapeDtypeStruct((2 * rows, 2 * wd.shape[0]), bf16),
        jax.ShapeDtypeStruct((wd.shape[0], 2 * rows), bf16),
        jax.ShapeDtypeStruct((width, 2 * rows), bf16),
        jax.ShapeDtypeStruct((2 * rows, LANES), bf16),
    )
    return pl.pallas_call(
        functools.partial(expert_backward_kernel, steps),
        out_shape=outs,
        grid=(steps,),
        in_specs=[ANYWHERE, first(width), second(width), first(width), second(width)]
        + [first(LANES), second(LANES), once(wr), once(wg), once(wu), once(wd)],
        out_specs=[first(width), second(width), whole(2 * wd.shape[0])]
        + [across(wd.shape[0]), across(width), whole(LANES)],
        compiler_params=params(),
        cost_estimate=cost(4 * rows * 5 * wg.size, 20e6),
        name="expert_backward",
    )(dep, *x, *gy, *sel, wr, wg, wu, wd)


def expert_weights(dep, xts, gys, acts, hids, glogs):
    pairs = len(xts)
    width = xts[0].shape[0]
    rows = acts[0].shape[0]
    local = hids[0].shape[0] // 128
    pair = 2 if pairs * rows <= 2048 else 1
    outs = (
        jax.ShapeDtypeStruct((local, width, 128), f32),
        jax.ShapeDtypeStruct((local, width, 128), f32),
        jax.ShapeDtypeStruct((local, 128, width), f32),
        jax.ShapeDtypeStruct((width, LANES), f32),
    )
    return pl.pallas_call(
        functools.partial(expert_weights_kernel, pairs),
        out_shape=outs,
        grid=(local // pair,),
        in_specs=[ANYWHERE]
        + [once(a) for a in xts]
        + [once(a) for a in gys]
        + [pl.BlockSpec((rows, 256 * pair), lambda i: (0, i))] * pairs
        + [pl.BlockSpec((128 * pair, rows), lambda i: (i, 0))] * pairs
        + [once(a) for a in glogs],
        out_specs=[
            pl.BlockSpec((pair, width, 128), lambda i: (i, 0, 0)),
            pl.BlockSpec((pair, width, 128), lambda i: (i, 0, 0)),
            pl.BlockSpec((pair, 128, width), lambda i: (i, 0, 0)),
            full(outs[3]),
        ],
        compiler_params=params(),
        cost_estimate=cost(2 * pairs * rows * width * 3 * 128 * local, 36e6),
        name="expert_weights",
    )(dep, *xts, *gys, *acts, *hids, *glogs)


def rms_scale(values):
    return lax.rsqrt(jnp.mean(values * values, axis=-1, keepdims=True) + EPSILON)


def norm_backward(grad_normed, values, scale_rows, gain):
    weighted = grad_normed * gain
    return scale_rows * weighted - values * scale_rows**3 * jnp.mean(
        values * weighted, axis=-1, keepdims=True
    )


def layout(lengths, row_ids):
    seq_ends = jnp.cumsum(lengths)
    starts = jnp.concatenate([seq_ends - lengths, seq_ends[-1:]])
    segment = jnp.sum((row_ids[:, None] >= seq_ends[None, :]).astype(jnp.int32), axis=1)
    picked = segment[:, None] == jnp.arange(SLOTS + 1, dtype=jnp.int32)[None, :]
    begins = jnp.sum(jnp.where(picked, starts[None, :], 0), axis=1)
    return (segment, (row_ids - begins).astype(f32))


def tables(position):
    frequency = THETA_BASE ** (-jnp.arange(0, HEAD_SIZE, 2, dtype=f32) / HEAD_SIZE)
    angles = position[:, None] * frequency[None, :]
    cosine, sine = jnp.cos(angles), jnp.sin(angles)
    cosine = jnp.concatenate([cosine] * 4, axis=-1)
    sine = jnp.concatenate([-sine, sine] * 2, axis=-1)
    return (cosine, sine)


def local(
    inputs,
    cotangent,
    seq_lengths,
    routes,
    gain_attn,
    w_query,
    key_projection,
    value_projection,
    w_out,
    gain_moe,
    w_router,
    w_gate,
    w_up,
    w_down,
):
    first = lax.axis_index("section") == 0
    e_no = lax.axis_index("expert")
    t_no = lax.axis_index("tensor")
    n_t = lax.axis_size("tensor")
    micro_count, rows, width = inputs.shape
    local_experts = w_gate.shape[1]
    micro = range(micro_count)
    part = rows // n_t

    gain_a = gain_attn.astype(f32)
    gain_m = gain_moe.astype(f32)
    wqkv = jnp.concatenate([w_query[0], key_projection[0], value_projection[0]], axis=1)
    wo = w_out[0]
    wr = jnp.pad(jnp.roll(w_router[0], -e_no * local_experts, axis=1), ((0, 0), (0, LANES - NE)))
    wg, wu = w_gate[0], w_up[0]
    wd = w_down[0].reshape(local_experts * 128, width)

    base = jnp.arange(rows, dtype=jnp.int32)
    row_ids = (((base // part) ^ t_no) * part) + base % part
    q_width = w_query.shape[2]

    def cut(array):
        blocks = array.reshape(micro_count, n_t, part, array.shape[2])
        return [
            lax.dynamic_index_in_dim(blocks, t_no ^ k, 1, keepdims=False).reshape(
                micro_count * part, array.shape[2]
            )
            for k in range(n_t)
        ]

    def joined(pieces):
        whole = jnp.stack([p.reshape(micro_count, part, p.shape[1]) for p in pieces], axis=1)
        return whole.reshape(micro_count * rows, pieces[0].shape[1])

    x_cut = cut(inputs)
    cot = cut(cotangent)[0]
    cosines, sines, masks, lives = [], [], [], []
    for m in micro:
        segment, position = layout(seq_lengths[m], row_ids)
        cosine, sine = tables(position)
        cosines.append(cosine)
        sines.append(sine)
        allowed = (segment[:, None] == segment[None, :]) & (row_ids[None, :] <= row_ids[:, None])
        masks.append(allowed.astype(f32))
        lives.append(segment < SLOTS)
    cosine, sine, mask = jnp.stack(cosines), jnp.stack(sines), jnp.stack(masks)
    named = jnp.where(jnp.concatenate(lives)[:, None], joined(cut(routes)), -1)
    shift = (jnp.arange(NE, dtype=jnp.int32) + e_no * local_experts) % NE
    shift = jnp.where(jnp.arange(LANES) < NE, jnp.pad(shift, (0, LANES - NE)), -2)

    def selected(block):
        return jnp.any(block[:, :, None] == shift[None, None, :], axis=1).astype(f32)

    wo_all = gather_weight(wo)

    def attend(dep, xs, wo_all):
        mixed, qkv, normed = attn_forward(dep, xs, gain_a, wqkv, q_width, cosine, sine, mask)
        block, middle = attn_project(
            qkv, pieces_tensor(mixed), xs, wo_all, gain_m, micro_count
        )
        return dict(xs=xs, qkv=qkv, mixed=mixed, normed=normed, middle=middle, block=block)

    def finish(saved, pieces, *done):
        return (saved["middle"] + reduce_pieces(pieces, *done)).astype(bf16)

    def experts(dep, j, saved):
        return expert_forward(dep, saved["rows"][j], sels[j], wr, wg, wu, wd)

    def experts_back(dep, j, saved, gathered):
        return expert_backward(dep, saved["rows"][j], gathered[j], sels[j], wr, wg, wu, wd)

    def mid_back(saved, grad_y, pieces, done):
        grad_normed = reduce_pieces(pieces, done)
        middle = saved["middle"]
        scale_mid = rms_scale(middle)
        g_gain_m = jnp.sum(grad_normed * middle * scale_mid, axis=0, keepdims=True)
        grad_middle = norm_backward(grad_normed, middle, scale_mid, gain_m) + grad_y.astype(f32)
        return (g_gain_m, grad_middle)

    def attend_back(dep, saved, grad_middle, gm_shard):
        parts, gqkv, g_gain_a, gm = attn_backward(
            dep, pieces_tensor(gm_shard), saved["xs"], saved["qkv"], wqkv, wo, cosine, sine, mask
        )
        grad_normed_in = reduce_pieces(parts)
        resid = saved["xs"][0].astype(f32)
        grad_in = norm_backward(grad_normed_in, resid, rms_scale(resid), gain_a) + grad_middle
        return (gqkv, jnp.sum(g_gain_a, axis=0), gm, grad_in.astype(bf16))

    def shared_grads(saved, gqkv, gm):
        return (dot_tn(saved["normed"], gqkv), dot_tn(saved["mixed"], gm))

    def expert_grads(dep, gathered, outs):
        return expert_weights(
            dep,
            [o[4] for o in outs],
            [g for both_cores in gathered for g in both_cores],
            [o[2] for o in outs],
            [o[3] for o in outs],
            [o[5] for o in outs],
        )

    saved0 = attend(wqkv, x_cut, wo_all)
    sels = [tuple(selected(p) for p in both_cores) for both_cores in gather_pairs(after(named, saved0["qkv"]))]
    pairs = range(len(sels))
    far = gather_far(saved0["block"])
    saved0["rows"] = [pair(far[0])]
    outs0 = [experts(saved0["middle"], 0, saved0)]
    for j in pairs[1:]:
        saved0["rows"].append(pair(after(far[j], outs0[0][0])))
        outs0.append(experts(outs0[j - 1][0], j, saved0))
    dep = outs0[-1][0]
    terms, sent = reduce_pairs(outs0)
    shard0 = finish(saved0, split_sum(dep, terms, n_t, micro_count))
    gathered1 = gather_pairs(joined(pieces_tensor(after(cot, saved0["qkv"]))))
    saved1 = attend(dep, pieces_tensor(shifted(shard0, 1)), wo_all)
    far = gather_far(saved1["block"])
    saved1["rows"] = [pair(far[0])]
    back_outs1 = [experts_back(saved1["middle"], 0, saved1, gathered1)]
    for j in pairs[1:]:
        saved1["rows"].append(pair(after(far[j], back_outs1[0][0])))
        back_outs1.append(experts_back(back_outs1[j - 1][5], j, saved1, gathered1))
    terms, sent = reduce_pairs([o[:2] for o in back_outs1])
    experts1 = expert_grads(sent, gathered1, back_outs1)
    pieces = split_sum(experts1[0], terms, n_t, micro_count)
    outs1 = [experts(pieces[0], 0, saved1)]
    g_gain_m1, grad_middle1 = mid_back(saved1, cot, pieces, outs1[0][0])
    gm_shard = grad_middle1.astype(bf16)
    dep = gm_shard
    for j in pairs[1:]:
        outs1.append(experts(dep, j, saved1))
        dep = outs1[j][0]
    gqkv1, g_gain_a1, gm1, grad_in1 = attend_back(dep, saved1, grad_middle1, gm_shard)
    terms1, sent = reduce_pairs(outs1)
    returned = shifted(grad_in1, -1)
    far = gather_far(joined(pieces_tensor(returned)))
    gathered0 = [pair(far[0])]
    back_outs0 = [experts_back(gqkv1, 0, saved0, gathered0)]
    dep = back_outs0[0][5]
    for j in pairs[1:]:
        gathered0.append(pair(after(far[j], back_outs0[0][5])))
        back_outs0.append(experts_back(dep, j, saved0, gathered0))
        dep = back_outs0[j][5]
    pieces1 = split_sum(dep, terms1, n_t, micro_count)
    terms, sent = reduce_pairs([o[:2] for o in back_outs0])
    g_gate, g_up, g_down, g_router = lax.cond(
        first,
        lambda: tuple(expert_grads(after(sent, pieces1[0]), gathered0, back_outs0)),
        lambda: tuple(experts1),
    )
    pieces = split_sum(g_gate, terms, n_t, micro_count)
    shard1 = finish(saved1, pieces1, g_gate)
    g_gain_m0, grad_middle0 = mid_back(saved0, returned, pieces, pieces[0])
    gqkv0, g_gain_a0, gm0, grad_in0 = attend_back(
        dep, saved0, grad_middle0, grad_middle0.astype(bf16)
    )
    g_qkv, g_out = (
        jnp.where(first, a, b)
        for a, b in zip(
            shared_grads(saved0, gqkv0, gm0),
            shared_grads(saved1, gqkv1, gm1),
        )
    )
    g_gains = jnp.concatenate(
        [jnp.where(first, g_gain_a0, g_gain_a1), jnp.where(first, g_gain_m0, g_gain_m1)], axis=0
    )
    g_qkv = sum_expert(g_qkv.astype(bf16)).astype(f32)
    g_out = sum_expert(g_out.astype(bf16)).astype(f32)
    g_gains = sum_all_small(g_gains)
    g_router = jnp.roll(g_router[:, :NE], e_no * local_experts, axis=1)
    g_router = lax.psum(g_router, ("expert", "tensor"))

    def assemble(shard, *done):
        blocks = pieces_tensor(shard)
        if done:
            blocks[-1] = after(blocks[-1], *done)
        blocks = [p.reshape(micro_count, part, width) for p in blocks]
        whole = relative(jnp.concatenate(blocks, axis=1), 1, t_no, n_t)
        return whole[None]

    activations = assemble(after(jnp.where(first, shard0, shard1), gqkv0))
    input_grads = assemble(jnp.where(first, grad_in0, grad_in1))
    kv_width = key_projection.shape[2]
    return (
        activations,
        input_grads,
        g_gains[:1],
        g_qkv[None, :, :q_width],
        g_qkv[None, :, q_width : q_width + kv_width],
        g_qkv[None, :, q_width + kv_width :],
        g_out[None],
        g_gains[1:],
        g_router[None],
        g_gate[None],
        g_up[None],
        g_down[None],
    )


def solution(mesh):
    in_specs = (
        P(None, "expert", None),
        P(None, "expert", None),
        P(None, "expert"),
        P(None, "expert", None),
        P("section", None),
        P("section", None, "tensor"),
        P("section", None, "tensor"),
        P("section", None, "tensor"),
        P("section", "tensor", None),
        P("section", None),
        P("section", None, None),
        P("section", "expert", None, "tensor"),
        P("section", "expert", None, "tensor"),
        P("section", "expert", "tensor", None),
    )
    out_specs = (
        P("section", None, "expert", None),
        P("section", None, "expert", None),
        P("section", None),
        P("section", None, "tensor"),
        P("section", None, "tensor"),
        P("section", None, "tensor"),
        P("section", "tensor", None),
        P("section", None),
        P("section", None, None),
        P("section", "expert", None, "tensor"),
        P("section", "expert", None, "tensor"),
        P("section", "expert", "tensor", None),
    )
    return jax.shard_map(local, mesh=mesh, in_specs=in_specs, out_specs=out_specs, check_vma=False)
```

time: 826 us -> 734 us (0.89)
  starting transfers between devices: 222 us -> 164 us
  local copies, waits for them, and re-layouts: 60.2 us -> 22.7 us
  waiting for transfers between devices: 210 us -> 241 us
  other arithmetic: 73.1 us -> 57 us
  matrix products: 19 us -> 3.92 us
  Pallas kernels: 215 us -> 228 us
    ppermute x151 -> x89, starting transfers between devices: 212 us -> 159 us  [swap(): lax.ppermute(x, axis, [(i, i ^ k) for i in range(lax.axis_size(axis))])]
    pallas_call x10 -> x16, Pallas kernels: 174 us -> 197 us  [the longest x4 84 us: expert_backward(): pl.pallas_call(functools.partial(expert_backward_kernel, steps), out_shap...]
    ppermute x151 -> x89, waiting for transfers between devices: 208 us -> 230 us  [swap(): lax.ppermute(x, axis, [(i, i ^ k) for i in range(lax.axis_size(axis))])]
    another operation x8 -> x3, local copies, waits for them, and re-layouts: 17.2 us -> 0.18 us  [joined(): jnp.stack([p.reshape(micro_count, part, p.shape[1]) for p in pieces], axi...]
    dot_general x16 -> x4, matrix products: 19 us -> 3.92 us  [dot_tn(): lax.dot_general(a, b, (((0,), (0,)), ((), ())), preferred_element_type=f32)]
    convert_element_type x24 -> x12, other arithmetic: 22.8 us -> 14.5 us  [the longest x4 8.2 us: added(): return sum((term.astype(f32) for term in terms)).astype(bf16)]
    pallas_call x4 -> x2, Pallas kernels: 17.9 us -> 12 us  [attn_forward(): pl.pallas_call(functools.partial(attn_forward_kernel, count), out_shape=o...]
    pallas_call x4 -> x2, Pallas kernels: 23.6 us -> 18.5 us  [attn_backward(): pl.pallas_call(functools.partial(attn_backward_kernel, count), out_shape=...]
  transfers between devices with their start and end apart: 156 -> 92, of which waited for: 52 -> 44; matrix products, arithmetic and copies ran while one was open for 15% -> 9% of each run, Pallas kernels for 16% -> 24%
where the time goes in v2:
time: 734 us; the launch traced here: 731 us
  waiting for transfers between devices  241 us (33%)
  Pallas kernels  228 us (31%)
  starting transfers between devices  164 us (22%)
  other arithmetic  57 us (8%)
  local copies, waits for them, and re-layouts  22.7 us (3%)
  between operations  15.4 us (2%)
    ppermute x89, waiting for transfers between devices, swap(): lax.ppermute(x, axis, [(i, i ^ k) for i in range(lax.axis_size(axis))])  230 us
    ppermute x89, starting transfers between devices, swap(): lax.ppermute(x, axis, [(i, i ^ k) for i in range(lax.axis_size(axis))])  159 us
    pallas_call x4, Pallas kernels, expert_backward(): pl.pallas_call(functools.partial(expert_backward_kernel, steps), out_shap...  84 us
    pallas_call x4, Pallas kernels, expert_forward(): pl.pallas_call(functools.partial(expert_forward_kernel, steps), out_shape...  50.6 us
    pallas_call x2, Pallas kernels, expert_weights(): pl.pallas_call(functools.partial(expert_weights_kernel, pairs), out_shape...  41.9 us
    pallas_call x2, Pallas kernels, attn_backward(): pl.pallas_call(functools.partial(attn_backward_kernel, count), out_shape=...  18.5 us
  transfers between devices with their start and end apart: 92, of which 44 were waited for; matrix products, arithmetic and copies ran while one was open for 9% of the time, Pallas kernels for 24%

profile of v2, /device:TPU:0, one launch (start us, length us, event | category | flops | bytes accessed | tf_op | source)
XLA Modules:
  0.0 731.4 jit_solution(11637658266303441625)
XLA Ops:
  53.0 10.4 %collective-permute-done.1.refs_3_ = bf16[512,256]{1,0:T(8,128)(2,1)} collective-permute-done((bf16[512,256]{1,0:T(8,128)(2,1)}, bf16[512,256]{1,0:T(8,128)(2,1)}, u32[]{:S(2)}, u32[]{:S(2)}) %collective-permute-start.1) | collective-permute-done | bytes 262176 | tf_op jit(solution)/shard_map/ppermute | solution.py:42
  79.8 12.6 %expert_forward.4 = (bf16[512,1024]{1,0:T(8,128)(2,1)}, bf16[512,1024]{1,0:T(8,128)(2,1)}) custom-call(f32[128,1024]{1,0:T(8,128)} %get-tuple-element.182.dep_ref, bf16[512,1024]{1,0:T(8,128)(2,1)} %get-tuple-element.183.xa_ref, bf16[512,1024]{1,0:T(8,128)(2,1)} %collective-permute-done.7.xb_ref, f32[512,128]{1,0:T(8,128)} %convert_element_type.261.sa_ref, ...), custom_call_target="tpu_custom_call" | custom-call | flops 6442450944 | bytes 12000000 | tf_op jit(solution)/shard_map/expert_forward/pallas_call | solution.py:541
  103.0 12.7 %expert_forward.5 = (bf16[512,1024]{1,0:T(8,128)(2,1)}, bf16[512,1024]{1,0:T(8,128)(2,1)}) custom-call(bf16[512,1024]{1,0:T(8,128)(2,1)} %get-tuple-element.185.dep_ref.refs_1_, bf16[512,1024]{1,0:T(8,128)(2,1)} %collective-permute-done.9.xa_ref, bf16[512,1024]{1,0:T(8,128)(2,1)} %copy-done.63, f32[512,128]{1,0:T(8,128)} %convert_element_type.263.sa_ref, ...), custom_call_target="tpu_custom_call" | custom-call | flops 6442450944 | bytes 12000000 | tf_op jit(solution)/shard_map/expert_forward/pallas_call | solution.py:541
  121.7 23.8 %collective-permute-done.15.refs_3_ = bf16[512,1024]{1,0:T(8,128)(2,1)} collective-permute-done((bf16[512,1024]{1,0:T(8,128)(2,1)S(1)}, bf16[512,1024]{1,0:T(8,128)(2,1)}, u32[]{:S(2)}, u32[]{:S(2)}) %collective-permute-start.15) | collective-permute-done | bytes 1048608 | tf_op jit(solution)/shard_map/ppermute | solution.py:42
  160.7 9.3 %collective-permute-done.17 = bf16[128,1024]{1,0:T(8,128)(2,1)S(1)} collective-permute-done((bf16[128,1024]{1,0:T(8,128)(2,1)}, bf16[128,1024]{1,0:T(8,128)(2,1)S(1)}, u32[]{:S(2)}, u32[]{:S(2)}) %collective-permute-start.17) | collective-permute-done | bytes 262176 | tf_op jit(solution)/shard_map/ppermute | solution.py:42
  188.7 19.2 %collective-permute-start.27 = (bf16[128,1024]{1,0:T(8,128)(2,1)S(1)}, bf16[128,1024]{1,0:T(8,128)(2,1)S(1)}, u32[]{:S(2)}, u32[]{:S(2)}) collective-permute-start(bf16[128,1024]{1,0:T(8,128)(2,1)S(1)} %bitcast.136), channel_id=1, source_target_pairs={{0,1},{1,0},{2,3},{3,2},{4,5},{5,4},{6,7},{7,6},{8,9},{9,8},{10,11... | collective-permute-start | bytes 786440 | tf_op jit(solution)/shard_map/ppermute | solution.py:42
  237.5 9.7 %collective-permute-done.24.refs_3_ = bf16[512,256]{1,0:T(8,128)(2,1)S(1)} collective-permute-done((bf16[512,256]{1,0:T(8,128)(2,1)}, bf16[512,256]{1,0:T(8,128)(2,1)S(1)}, u32[]{:S(2)}, u32[]{:S(2)}) %collective-permute-start.24) | collective-permute-done | bytes 262176 | tf_op jit(solution)/shard_map/ppermute | solution.py:42
  255.8 21.0 %expert_backward.4 = (bf16[512,1024]{1,0:T(8,128)(2,1)}, bf16[512,1024]{1,0:T(8,128)(2,1)}, bf16[1024,2048]{1,0:T(8,128)(2,1)}, bf16[1024,1024]{1,0:T(8,128)(2,1...) custom-call(f32[128,1024]{1,0:T(8,128)} %get-tuple-element.196.dep_ref, ...), custom_call_target="tpu_custom_call" | custom-call | flops 10737418240 | bytes 20000000 | tf_op jit(solution)/shard_map/expert_backward/pallas_call | solution.py:567
  282.5 21.0 %expert_backward.5 = (bf16[512,1024]{1,0:T(8,128)(2,1)}, bf16[512,1024]{1,0:T(8,128)(2,1)}, bf16[1024,2048]{1,0:T(8,128)(2,1)}, bf16[1024,1024]{1,0:T(8,128)(2,1...) custom-call(bf16[1024,128]{1,0:T(8,128)(2,1)} %get-tuple-element.199.dep_ref.refs_11_, ...), custom_call_target="tpu_custom_call" | custom-call | flops 10737418240 | bytes 20000000 | tf_op jit(solution)/shard_map/expert_backward/pallas_call | solution.py:567
  310.8 21.2 %expert_weights.4 = (f32[8,1024,128]{2,1,0:T(8,128)}, f32[8,1024,128]{2,1,0:T(8,128)}, f32[8,128,1024]{2,1,0:T(8,128)}, f32[1024,128]{1,0:T(8,128)}) custom-call(bf16[512,1024]{1,0:T(8,128)(2,1)} %add_convert_fusion.2.refs_0_, bf16[1024,1024]{1,0:T(8,128)(2,1)} %get-tuple-element.204.refs_1_, bf16[1024,1024]{1,0:T(8,128)(2,1)} %get-tuple-element.205.refs_2_, ...), custom_call_target="tpu_custom_call" | custom-call | flops 12884901888 | bytes 36000000 | tf_op jit(solution)/shard_map/expert_weights/pallas_call | solution.py:593
  341.8 12.7 %expert_forward.6 = (bf16[512,1024]{1,0:T(8,128)(2,1)}, bf16[512,1024]{1,0:T(8,128)(2,1)}) custom-call(bf16[128,1024]{1,0:T(8,128)(2,1)} %get-tuple-element.213.dep_ref, bf16[512,1024]{1,0:T(8,128)(2,1)} %get-tuple-element.197.xa_ref, bf16[512,1024]{1,0:T(8,128)(2,1)} %collective-permute-done.26.xb_ref, f32[512,128]{1,0:T(8,128)} %convert_element_type.261.sa_ref, ...), custom_call_target="tpu_custom_call" | custom-call | flops 6442450944 | bytes 12000000 | tf_op jit(solution)/shard_map/expert_forward/pallas_call | solution.py:541
  361.9 12.1 %collective-permute-start.42 = (bf16[128,1024]{1,0:T(8,128)(2,1)S(1)}, bf16[128,1024]{1,0:T(8,128)(2,1)S(1)}, u32[]{:S(2)}, u32[]{:S(2)}) collective-permute-start(bf16[128,1024]{1,0:T(8,128)(2,1)S(1)} %get-tuple-element.283.dep_ref.refs_1_), channel_id=1, source_target_pairs={{0,2},{1,3},{2,0},{3,1},{4,6},{5,7},{6,4},{7,5},{8,10},{9,11},{10,... | collective-permute-start | bytes 786440 | tf_op jit(solution)/shard_map/ppermute | solution.py:42
  374.5 12.6 %expert_forward.7 = (bf16[512,1024]{1,0:T(8,128)(2,1)}, bf16[512,1024]{1,0:T(8,128)(2,1)}) custom-call(bf16[128,1024]{1,0:T(8,128)(2,1)} %copy-done.27, bf16[512,1024]{1,0:T(8,128)(2,1)} %copy-done.66, bf16[512,1024]{1,0:T(8,128)(2,1)} %copy-done.67, f32[512,128]{1,0:T(8,128)} %convert_element_type.263.sa_ref, f32[512,128]{1,0:T(8,128)} %convert_element_type.264.sb_ref, ...), custom_call_target="tpu_custom_call" | custom-call | flops 6442450944 | bytes 12000000 | tf_op jit(solution)/shard_map/expert_forward/pallas_call | solution.py:541
  435.5 9.7 %collective-permute-done.49 = bf16[128,1024]{1,0:T(8,128)(2,1)S(1)} collective-permute-done((bf16[128,1024]{1,0:T(8,128)(2,1)S(1)}, bf16[128,1024]{1,0:T(8,128)(2,1)S(1)}, u32[]{:S(2)}, u32[]{:S(2)}) %collective-permute-start.49) | collective-permute-done | bytes 262176 | tf_op jit(solution)/shard_map/ppermute | solution.py:42
  450.4 21.0 %expert_backward.6 = (bf16[512,1024]{1,0:T(8,128)(2,1)}, bf16[512,1024]{1,0:T(8,128)(2,1)}, bf16[1024,2048]{1,0:T(8,128)(2,1)}, bf16[1024,1024]{1,0:T(8,128)(2,1...) custom-call(bf16[512,512]{1,0:T(8,128)(2,1)} %get-tuple-element.220.dep_ref, ...), custom_call_target="tpu_custom_call" | custom-call | flops 10737418240 | bytes 20000000 | tf_op jit(solution)/shard_map/expert_backward/pallas_call | solution.py:567
  476.3 21.0 %expert_backward.7 = (bf16[512,1024]{1,0:T(8,128)(2,1)}, bf16[512,1024]{1,0:T(8,128)(2,1)}, bf16[1024,2048]{1,0:T(8,128)(2,1)}, bf16[1024,1024]{1,0:T(8,128)(2,1...) custom-call(bf16[1024,128]{1,0:T(8,128)(2,1)S(1)} %get-tuple-element.225.dep_ref, ...), custom_call_target="tpu_custom_call" | custom-call | flops 10737418240 | bytes 20000000 | tf_op jit(solution)/shard_map/expert_backward/pallas_call | solution.py:567
  504.0 22.8 %collective-permute-done.56.refs_3_ = bf16[512,1024]{1,0:T(8,128)(2,1)} collective-permute-done((bf16[512,1024]{1,0:T(8,128)(2,1)}, bf16[512,1024]{1,0:T(8,128)(2,1)}, u32[]{:S(2)}, u32[]{:S(2)}) %collective-permute-start.56) | collective-permute-done | bytes 1048608 | tf_op jit(solution)/shard_map/ppermute | solution.py:42
  530.8 25.2 %conditional.1 = (f32[8,1024,128]{2,1,0:T(8,128)}, f32[1024,128]{1,0:T(8,128)}, f32[1,8,1024,128]{3,2,1,0:T(8,128)}, f32[1,8,1024,128]{3,2,1,0:T(8,128)}, f32[1,8,128,1024]{3,2,1,0:T(8,128)}) conditional(s32[]{:T(128)} %convert_element_type.294, (f32[8,1024,128]{2,1,0:T(8,128)}, f32[8,1024,128]{2,1,0:T(8,128)}, f32[8,128,1024]{2,1,0:T(8,128)}, ...), branch_computations={%region_14.15_spmd, %region_15.16_spmd} | conditional | flops 12884901888 | bytes 44388648 | solution.py:804
  530.8 20.7 %expert_weights.3 = (f32[8,1024,128]{2,1,0:T(8,128)}, f32[8,1024,128]{2,1,0:T(8,128)}, f32[8,128,1024]{2,1,0:T(8,128)}, f32[1024,128]{1,0:T(8,128)}) custom-call(bf16[512,1024]{1,0:T(8,128)(2,1)} %get-tuple-element.64.refs_0_, bf16[1024,1024]{1,0:T(8,128)(2,1)} %get-tuple-element.65.refs_1_, bf16[1024,1024]{1,0:T(8,128)(2,1)} %get-tuple-element.66.refs_2_, ...), custom_call_target="tpu_custom_call" | custom-call | flops 12884901888 | bytes 36000000 | tf_op jit(solution)/shard_map/cond/branch_1_fun/expert_weights/pallas_call | solution.py:593
  570.1 11.5 %collective-permute-done.65 = bf16[128,1024]{1,0:T(8,128)(2,1)S(1)} collective-permute-done((bf16[128,1024]{1,0:T(8,128)(2,1)}, bf16[128,1024]{1,0:T(8,128)(2,1)S(1)}, u32[]{:S(2)}, u32[]{:S(2)}) %collective-permute-start.65) | collective-permute-done | bytes 262176 | tf_op jit(solution)/shard_map/ppermute | solution.py:42
  587.3 20.1 %collective-permute-start.67 = (bf16[128,1024]{1,0:T(8,128)(2,1)S(1)}, bf16[128,1024]{1,0:T(8,128)(2,1)S(1)}, u32[]{:S(2)}, u32[]{:S(2)}) collective-permute-start(bf16[128,1024]{1,0:T(8,128)(2,1)S(1)} %get-tuple-element.281.refs_1_), channel_id=1, source_target_pairs={{0,2},{1,3},{2,0},{3,1},{4,6},{5,7},{6,4},{7,5},{8,10},{9,11},{10,... | collective-permute-start | bytes 786440 | tf_op jit(solution)/shard_map/ppermute | solution.py:42
  609.8 10.0 %collective-permute-done.67.refs_3_ = bf16[128,1024]{1,0:T(8,128)(2,1)S(1)} collective-permute-done((bf16[128,1024]{1,0:T(8,128)(2,1)S(1)}, bf16[128,1024]{1,0:T(8,128)(2,1)S(1)}, u32[]{:S(2)}, u32[]{:S(2)}) %collective-permute-start.67) | collective-permute-done | bytes 262176 | tf_op jit(solution)/shard_map/ppermute | solution.py:42
  656.0 17.3 %collective-permute-done.73 = bf16[128,1024]{1,0:T(8,128)(2,1)S(1)} collective-permute-done((bf16[128,1024]{1,0:T(8,128)(2,1)S(1)}, bf16[128,1024]{1,0:T(8,128)(2,1)S(1)}, u32[]{:S(2)}, u32[]{:S(2)}) %collective-permute-start.73) | collective-permute-done | bytes 262176 | tf_op jit(solution)/shard_map/ppermute | solution.py:42
  682.5 13.5 %collective-permute-done.70 = bf16[128,1024]{1,0:T(8,128)(2,1)S(1)} collective-permute-done((bf16[128,1024]{1,0:T(8,128)(2,1)S(1)}, bf16[128,1024]{1,0:T(8,128)(2,1)S(1)}, u32[]{:S(2)}, u32[]{:S(2)}) %collective-permute-start.70) | collective-permute-done | bytes 262176 | tf_op jit(solution)/shard_map/ppermute | solution.py:42
  (456 shorter events, 350.2 us)
Async XLA Ops:
  7.2 715.6 %all-reduce.4.cloned.1.call-start = ((), (), s32[]{:S(2)}) async-start(), calls=%async_computation | async-start | bytes 262144 | tf_op jit(solution)/shard_map/psum | solution.py:829
  9.2 33.1 %collective-permute-start.5 = (bf16[128,1024]{1,0:T(8,128)(2,1)}, bf16[128,1024]{1,0:T(8,128)(2,1)S(1)}, u32[]{:S(2)}, u32[]{:S(2)}) collective-permute-start(bf16[128,1024]{1,0:T(8,128)(2,1)} %select_bitcast_fusion.2), channel_id=1, source_target_pairs={{0,3},{1,2},{2,1},{3,0},{4,7},{5,6},{6,5},{7,4},{8,11},{9,10},{10,... | collective-permute-start | bytes 786440 | tf_op jit(solution)/shard_map/ppermute | solution.py:42
  14.2 28.8 %collective-permute-start.4 = (bf16[128,1024]{1,0:T(8,128)(2,1)}, bf16[128,1024]{1,0:T(8,128)(2,1)S(1)}, u32[]{:S(2)}, u32[]{:S(2)}) collective-permute-start(bf16[128,1024]{1,0:T(8,128)(2,1)} %select_bitcast_fusion.2), channel_id=1, source_target_pairs={{0,2},{1,3},{2,0},{3,1},{4,6},{5,7},{6,4},{7,5},{8,10},{9,11},{10,... | collective-permute-start | bytes 786440 | tf_op jit(solution)/shard_map/ppermute | solution.py:42
  14.2 28.8 %collective-permute-start.3 = (bf16[128,1024]{1,0:T(8,128)(2,1)}, bf16[128,1024]{1,0:T(8,128)(2,1)S(1)}, u32[]{:S(2)}, u32[]{:S(2)}) collective-permute-start(bf16[128,1024]{1,0:T(8,128)(2,1)} %select_bitcast_fusion.2), channel_id=1, source_target_pairs={{0,1},{1,0},{2,3},{3,2},{4,5},{5,4},{6,7},{7,6},{8,9},{9,8},{10,11... | collective-permute-start | bytes 786440 | tf_op jit(solution)/shard_map/ppermute | solution.py:42
  180.8 34.0 %collective-permute-start.21 = (bf16[128,1024]{1,0:T(8,128)(2,1)S(1)}, bf16[128,1024]{1,0:T(8,128)(2,1)S(1)}, u32[]{:S(2)}, u32[]{:S(2)}) collective-permute-start(bf16[128,1024]{1,0:T(8,128)(2,1)S(1)} %collective-permute-done.19.refs_1_.refs_5_), channel_id=1, source_target_pairs={{0,2},{1,3},{2,0},{3,1},{4,6},{5,7},{6,4},{7,5},{8,10},{9,11},{10,... | collective-permute-start | bytes 786440 | tf_op jit(solution)/shard_map/ppermute | solution.py:42
  184.7 30.2 %collective-permute-start.20 = (bf16[128,1024]{1,0:T(8,128)(2,1)S(1)}, bf16[128,1024]{1,0:T(8,128)(2,1)S(1)}, u32[]{:S(2)}, u32[]{:S(2)}) collective-permute-start(bf16[128,1024]{1,0:T(8,128)(2,1)S(1)} %collective-permute-done.19.refs_1_.refs_5_), channel_id=1, source_target_pairs={{0,1},{1,0},{2,3},{3,2},{4,5},{5,4},{6,7},{7,6},{8,9},{9,8},{10,11... | collective-permute-start | bytes 786440 | tf_op jit(solution)/shard_map/ppermute | solution.py:42
  184.7 39.9 %collective-permute-start.29 = (bf16[128,1024]{1,0:T(8,128)(2,1)S(1)}, bf16[128,1024]{1,0:T(8,128)(2,1)S(1)}, u32[]{:S(2)}, u32[]{:S(2)}) collective-permute-start(bf16[128,1024]{1,0:T(8,128)(2,1)S(1)} %bitcast.134), channel_id=1, source_target_pairs={{0,3},{1,2},{2,1},{3,0},{4,7},{5,6},{6,5},{7,4},{8,11},{9,10},{10,... | collective-permute-start | bytes 786440 | tf_op jit(solution)/shard_map/ppermute | solution.py:42
  187.2 48.4 %collective-permute-start.28 = (bf16[128,1024]{1,0:T(8,128)(2,1)S(1)}, bf16[128,1024]{1,0:T(8,128)(2,1)S(1)}, u32[]{:S(2)}, u32[]{:S(2)}) collective-permute-start(bf16[128,1024]{1,0:T(8,128)(2,1)S(1)} %bitcast.135), channel_id=1, source_target_pairs={{0,2},{1,3},{2,0},{3,1},{4,6},{5,7},{6,4},{7,5},{8,10},{9,11},{10,... | collective-permute-start | bytes 786440 | tf_op jit(solution)/shard_map/ppermute | solution.py:42
  188.7 46.8 %collective-permute-start.27 = (bf16[128,1024]{1,0:T(8,128)(2,1)S(1)}, bf16[128,1024]{1,0:T(8,128)(2,1)S(1)}, u32[]{:S(2)}, u32[]{:S(2)}) collective-permute-start(bf16[128,1024]{1,0:T(8,128)(2,1)S(1)} %bitcast.136), channel_id=1, source_target_pairs={{0,1},{1,0},{2,3},{3,2},{4,5},{5,4},{6,7},{7,6},{8,9},{9,8},{10,11... | collective-permute-start | bytes 786440 | tf_op jit(solution)/shard_map/ppermute | solution.py:42
  303.8 28.2 %collective-permute-start.36 = (bf16[512,1024]{1,0:T(8,128)(2,1)}, bf16[512,1024]{1,0:T(8,128)(2,1)S(1)}, u32[]{:S(2)}, u32[]{:S(2)}) collective-permute-start(bf16[512,1024]{1,0:T(8,128)(2,1)} %get-tuple-element.212), channel_id=1, source_target_pairs={{0,4},{4,0},{8,12},{12,8},{1,5},{5,1},{9,13},{13,9},{2,6},{6,2},{1... | collective-permute-start | bytes 3145736 | tf_op jit(solution)/shard_map/ppermute | solution.py:42
  502.2 53.7 %collective-permute-start.61 = (bf16[512,1024]{1,0:T(8,128)(2,1)}, bf16[512,1024]{1,0:T(8,128)(2,1)S(1)}, u32[]{:S(2)}, u32[]{:S(2)}) collective-permute-start(bf16[512,1024]{1,0:T(8,128)(2,1)} %get-tuple-element.245), channel_id=1, source_target_pairs={{0,4},{4,0},{8,12},{12,8},{1,5},{5,1},{9,13},{13,9},{2,6},{6,2},{1... | collective-permute-start | bytes 3145736 | tf_op jit(solution)/shard_map/ppermute | solution.py:42
  503.6 52.3 %collective-permute-start.62 = (bf16[512,1024]{1,0:T(8,128)(2,1)}, bf16[512,1024]{1,0:T(8,128)(2,1)}, u32[]{:S(2)}, u32[]{:S(2)}) collective-permute-start(bf16[512,1024]{1,0:T(8,128)(2,1)} %add_convert_fusion), channel_id=1, source_target_pairs={{0,8},{4,12},{8,0},{12,4},{1,9},{5,13},{9,1},{13,5},{2,10},{6,14},... | collective-permute-start | bytes 3145736 | tf_op jit(solution)/shard_map/ppermute | solution.py:42
  529.6 37.3 %collective-permute-start.59 = (bf16[128,1024]{1,0:T(8,128)(2,1)}, bf16[128,1024]{1,0:T(8,128)(2,1)}, u32[]{:S(2)}, u32[]{:S(2)}) collective-permute-start(bf16[128,1024]{1,0:T(8,128)(2,1)} %get-tuple-element.233), channel_id=1, source_target_pairs={{0,3},{1,2},{2,1},{3,0},{4,7},{5,6},{6,5},{7,4},{8,11},{9,10},{10,... | collective-permute-start | bytes 786440 | tf_op jit(solution)/shard_map/ppermute | solution.py:42
  564.4 42.9 %collective-permute-start.57 = (bf16[128,1024]{1,0:T(8,128)(2,1)}, bf16[128,1024]{1,0:T(8,128)(2,1)}, u32[]{:S(2)}, u32[]{:S(2)}) collective-permute-start(bf16[128,1024]{1,0:T(8,128)(2,1)} %get-tuple-element.231), channel_id=1, source_target_pairs={{0,1},{1,0},{2,3},{3,2},{4,5},{5,4},{6,7},{7,6},{8,9},{9,8},{10,11... | collective-permute-start | bytes 786440 | tf_op jit(solution)/shard_map/ppermute | solution.py:42
  566.9 41.6 %collective-permute-start.58 = (bf16[128,1024]{1,0:T(8,128)(2,1)}, bf16[128,1024]{1,0:T(8,128)(2,1)}, u32[]{:S(2)}, u32[]{:S(2)}) collective-permute-start(bf16[128,1024]{1,0:T(8,128)(2,1)} %get-tuple-element.232), channel_id=1, source_target_pairs={{0,2},{1,3},{2,0},{3,1},{4,6},{5,7},{6,4},{7,5},{8,10},{9,11},{10,... | collective-permute-start | bytes 786440 | tf_op jit(solution)/shard_map/ppermute | solution.py:42
  587.3 32.5 %collective-permute-start.67 = (bf16[128,1024]{1,0:T(8,128)(2,1)S(1)}, bf16[128,1024]{1,0:T(8,128)(2,1)S(1)}, u32[]{:S(2)}, u32[]{:S(2)}) collective-permute-start(bf16[128,1024]{1,0:T(8,128)(2,1)S(1)} %get-tuple-element.281.refs_1_), channel_id=1, source_target_pairs={{0,2},{1,3},{2,0},{3,1},{4,6},{5,7},{6,4},{7,5},{8,10},{9,11},{10,... | collective-permute-start | bytes 786440 | tf_op jit(solution)/shard_map/ppermute | solution.py:42
  638.5 39.8 %collective-permute-start.71 = (bf16[128,1024]{1,0:T(8,128)(2,1)S(1)}, bf16[128,1024]{1,0:T(8,128)(2,1)S(1)}, u32[]{:S(2)}, u32[]{:S(2)}) collective-permute-start(bf16[128,1024]{1,0:T(8,128)(2,1)S(1)} %fusion.12), channel_id=1, source_target_pairs={{0,3},{1,2},{2,1},{3,0},{4,7},{5,6},{6,5},{7,4},{8,11},{9,10},{10,... | collective-permute-start | bytes 786440 | tf_op jit(solution)/shard_map/ppermute | solution.py:42
  642.8 30.5 %collective-permute-start.73 = (bf16[128,1024]{1,0:T(8,128)(2,1)S(1)}, bf16[128,1024]{1,0:T(8,128)(2,1)S(1)}, u32[]{:S(2)}, u32[]{:S(2)}) collective-permute-start(bf16[128,1024]{1,0:T(8,128)(2,1)S(1)} %copy-done.70), channel_id=1, source_target_pairs={{0,2},{1,3},{2,0},{3,1},{4,6},{5,7},{6,4},{7,5},{8,10},{9,11},{10,... | collective-permute-start | bytes 786440 | tf_op jit(solution)/shard_map/ppermute | solution.py:42
  644.8 28.5 %collective-permute-start.74 = (bf16[128,1024]{1,0:T(8,128)(2,1)S(1)}, bf16[128,1024]{1,0:T(8,128)(2,1)S(1)}, u32[]{:S(2)}, u32[]{:S(2)}) collective-permute-start(bf16[128,1024]{1,0:T(8,128)(2,1)S(1)} %copy-done.69), channel_id=1, source_target_pairs={{0,3},{1,2},{2,1},{3,0},{4,7},{5,6},{6,5},{7,4},{8,11},{9,10},{10,... | collective-permute-start | bytes 786440 | tf_op jit(solution)/shard_map/ppermute | solution.py:42
  652.2 43.8 %collective-permute-start.70 = (bf16[128,1024]{1,0:T(8,128)(2,1)S(1)}, bf16[128,1024]{1,0:T(8,128)(2,1)S(1)}, u32[]{:S(2)}, u32[]{:S(2)}) collective-permute-start(bf16[128,1024]{1,0:T(8,128)(2,1)S(1)} %fusion.12), channel_id=1, source_target_pairs={{0,2},{1,3},{2,0},{3,1},{4,6},{5,7},{6,4},{7,5},{8,10},{9,11},{10,... | collective-permute-start | bytes 786440 | tf_op jit(solution)/shard_map/ppermute | solution.py:42
  653.5 42.9 %collective-permute-start.69 = (bf16[128,1024]{1,0:T(8,128)(2,1)S(1)}, bf16[128,1024]{1,0:T(8,128)(2,1)S(1)}, u32[]{:S(2)}, u32[]{:S(2)}) collective-permute-start(bf16[128,1024]{1,0:T(8,128)(2,1)S(1)} %fusion.12), channel_id=1, source_target_pairs={{0,1},{1,0},{2,3},{3,2},{4,5},{5,4},{6,7},{7,6},{8,9},{9,8},{10,11... | collective-permute-start | bytes 786440 | tf_op jit(solution)/shard_map/ppermute | solution.py:42
  673.3 30.9 %collective-permute-start.83 = (bf16[512,512]{1,0:T(8,128)(2,1)S(1)}, bf16[512,512]{1,0:T(8,128)(2,1)S(1)}, u32[]{:S(2)}, u32[]{:S(2)}) collective-permute-start(bf16[512,512]{1,0:T(8,128)(2,1)S(1)} %broadcast_select_fusion.2), channel_id=1, source_target_pairs={{0,4},{4,0},{8,12},{12,8},{1,5},{5,1},{9,13},{13,9},{2,6},{6,2},{1... | collective-permute-start | bytes 1572872 | tf_op jit(solution)/shard_map/ppermute | solution.py:42
  674.9 32.7 %collective-permute-start.77 = (bf16[128,1024]{1,0:T(8,128)(2,1)S(1)}, bf16[128,1024]{1,0:T(8,128)(2,1)S(1)}, u32[]{:S(2)}, u32[]{:S(2)}) collective-permute-start(bf16[128,1024]{1,0:T(8,128)(2,1)S(1)} %fusion.13), channel_id=1, source_target_pairs={{0,3},{1,2},{2,1},{3,0},{4,7},{5,6},{6,5},{7,4},{8,11},{9,10},{10,... | collective-permute-start | bytes 786440 | tf_op jit(solution)/shard_map/ppermute | solution.py:42
  678.3 29.3 %collective-permute-start.76 = (bf16[128,1024]{1,0:T(8,128)(2,1)S(1)}, bf16[128,1024]{1,0:T(8,128)(2,1)S(1)}, u32[]{:S(2)}, u32[]{:S(2)}) collective-permute-start(bf16[128,1024]{1,0:T(8,128)(2,1)S(1)} %fusion.13), channel_id=1, source_target_pairs={{0,2},{1,3},{2,0},{3,1},{4,6},{5,7},{6,4},{7,5},{8,10},{9,11},{10,... | collective-permute-start | bytes 786440 | tf_op jit(solution)/shard_map/ppermute | solution.py:42
  (140 other events, 1914.8 us)
Sparse Core Ops, SparseCore 0:
  570.2 105.0 all-reduce.3
